TPU v7x, 256 devices: a whole 4x4x8 slice. The times are simulated.
256 devices in a mesh: ctx: 32 (over y, x, core), head: 8 (over z).
Axes of the slice: x: 4, y: 4, z: 8, core: 2. Of those that a mesh axis runs over, the one named last changes fastest.
Arguments:
- queries: bfloat16 [32768, 4096], P(('ctx', 'head')), may hold values from -81 to 81
- keys: bfloat16 [32768, 1024], P(('ctx', 'head')), may hold values from -4.05 to 4.05
- values: bfloat16 [32768, 1024], P(('ctx', 'head')), may hold values from -6 to 6
- output_gradient: bfloat16 [32768, 4096], P(('ctx', 'head')), may hold values from -6 to 6
- doc_lengths: int32 [64], replicated, may hold values from 1 to 2048, 32768 in all
Outputs:
- attended: bfloat16 [32768, 4096], P(('ctx', 'head'))
- grad_queries: bfloat16 [32768, 4096], P(('ctx', 'head'))
- key_gradient: bfloat16 [32768, 1024], P(('ctx', 'head'))
- value_gradient: bfloat16 [32768, 1024], P(('ctx', 'head'))
Inputs may be any that keep to these rules, and one draw needn't show every extreme that they name: `doc_lengths`: their sum is 32768; one document has exactly 2048 tokens.
All inputs are finite; a program needn't handle non-finite values.
Results may differ from a plain program's by a relative error of at most 0.039.
Values may be sent and summed in bfloat16 or wider, within the bound.
A program may use at most 192 MiB of HBM per device.

v0:
```python
import jax
import jax.numpy as jnp
from jax import lax
from jax.sharding import PartitionSpec as P

HEAD_SIZE = 128
REACH = 2


def from_behind(array, axis, by):
    length = lax.axis_size(axis)
    pairs = [(i, i + by) for i in range(length) if 0 <= i + by < length]
    return lax.ppermute(array, axis, pairs)


def document_ids(doc_ends, positions):
    counted = jnp.sum((doc_ends[None, :] <= positions[:, None]).astype(jnp.int32), axis=1)
    return jnp.where(positions < 0, -1, counted)


def window_of(array, offset, length, reduce_axis):
    return lax.dynamic_slice_in_dim(array, offset, length, reduce_axis)


def masked_scores(query_block, key_block, query_doc, key_doc, query_pos, key_pos):
    scores = jnp.einsum(
        "qhgd,khd->hgqk", query_block, key_block, preferred_element_type=jnp.float32
    ) * HEAD_SIZE ** (-0.5)
    allowed = (query_doc[:, None] == key_doc[None, :]) & (key_pos[None, :] <= query_pos[:, None])
    return jnp.where(allowed, scores, -jnp.inf)


def touches(query_doc, key_doc, query_pos, key_pos):
    return (
        (key_pos[0] <= query_pos[-1])
        & (key_doc[-1] >= query_doc[0])
        & (key_doc[0] <= query_doc[-1])
    )


def attend(
    query_rows_4d, query_pos, query_doc, key_rows_3d, value_rows_3d, key_pos, key_doc, tile_rows
):
    head_count = query_rows_4d.shape[1]
    query_group_width = query_rows_4d.shape[2]
    key_tiles = key_rows_3d.shape[0] // tile_rows

    def attend_one_block(offset):
        query_block = window_of(query_rows_4d, offset, tile_rows, 0)
        query_place = window_of(query_pos, offset, tile_rows, 0)
        query_label = window_of(query_doc, offset, tile_rows, 0)

        def key_tile(number):
            first = number * tile_rows
            return (
                window_of(key_rows_3d, first, tile_rows, 0),
                window_of(value_rows_3d, first, tile_rows, 0),
                window_of(key_pos, first, tile_rows, 0),
                window_of(key_doc, first, tile_rows, 0),
            )

        empty_tile = jnp.full(
            (head_count, query_group_width, tile_rows, tile_rows), -jnp.inf, jnp.float32
        )

        def score_tile(number, stored):
            key_block, value_block, key_place, key_label = key_tile(number)
            tile_scores = lax.cond(
                touches(query_label, key_label, query_place, key_place),
                lambda: masked_scores(
                    query_block, key_block, query_label, key_label, query_place, key_place
                ),
                lambda: empty_tile,
            )
            return lax.dynamic_update_index_in_dim(stored, tile_scores, number, 0)

        stored = lax.fori_loop(
            0,
            key_tiles,
            score_tile,
            jnp.full(
                (key_tiles, head_count, query_group_width, tile_rows, tile_rows),
                -jnp.inf,
                jnp.float32,
            ),
        )
        row_max = jnp.max(stored, axis=(0, 4))
        row_sum = jnp.sum(jnp.exp(stored - row_max[None, ..., None]), axis=(0, 4))
        log_total = row_max + jnp.log(row_sum)

        def gather_out(number, carried):
            key_block, value_block, key_place, key_label = key_tile(number)

            def gather_update(running):
                scores = lax.dynamic_index_in_dim(stored, number, 0, keepdims=False)
                weights = jnp.exp(scores - log_total[..., None]).astype(jnp.bfloat16)
                return running + jnp.einsum(
                    "hgqk,khd->qhgd", weights, value_block, preferred_element_type=jnp.float32
                )

            return lax.cond(
                touches(query_label, key_label, query_place, key_place),
                gather_update,
                lambda unchanged: unchanged,
                carried,
            )

        summed = lax.fori_loop(
            0,
            key_tiles,
            gather_out,
            jnp.zeros((tile_rows, head_count, query_group_width, HEAD_SIZE), jnp.float32),
        )
        return (log_total, summed.astype(jnp.bfloat16))

    offsets = jnp.arange(query_rows_4d.shape[0] // tile_rows, dtype=jnp.int32) * tile_rows
    log_total, attended = lax.map(attend_one_block, offsets)
    log_total = jnp.moveaxis(log_total, 0, 2).reshape(head_count, query_group_width, -1)
    return (log_total, attended.reshape(query_rows_4d.shape))


def query_grads(
    query_rows_4d,
    output_gradient_4d,
    query_pos,
    query_doc,
    log_total,
    row_delta,
    key_rows_3d,
    value_rows_3d,
    key_pos,
    key_doc,
    tile_rows,
):
    head_count = query_rows_4d.shape[1]
    query_group_width = query_rows_4d.shape[2]
    key_tiles = key_rows_3d.shape[0] // tile_rows

    def query_one_block(offset):
        query_block = window_of(query_rows_4d, offset, tile_rows, 0)
        grad_block = window_of(output_gradient_4d, offset, tile_rows, 0)
        query_place = window_of(query_pos, offset, tile_rows, 0)
        query_label = window_of(query_doc, offset, tile_rows, 0)
        total_block = window_of(log_total, offset, tile_rows, 2)
        delta_block = window_of(row_delta, offset, tile_rows, 2)

        def query_gather_terms(number, carried):
            first = number * tile_rows
            key_block = window_of(key_rows_3d, first, tile_rows, 0)
            value_block = window_of(value_rows_3d, first, tile_rows, 0)
            key_place = window_of(key_pos, first, tile_rows, 0)
            key_label = window_of(key_doc, first, tile_rows, 0)

            def query_update(running):
                scores = masked_scores(
                    query_block, key_block, query_label, key_label, query_place, key_place
                )
                prob = jnp.exp(scores - total_block[..., None])
                grad_weights = jnp.einsum(
                    "qhgd,khd->hgqk", grad_block, value_block, preferred_element_type=jnp.float32
                )
                grad_scores = (prob * (grad_weights - delta_block[..., None])).astype(jnp.bfloat16)
                return running + jnp.einsum(
                    "hgqk,khd->qhgd", grad_scores, key_block, preferred_element_type=jnp.float32
                )

            return lax.cond(
                touches(query_label, key_label, query_place, key_place),
                query_update,
                lambda unchanged: unchanged,
                carried,
            )

        summed = lax.fori_loop(
            0,
            key_tiles,
            query_gather_terms,
            jnp.zeros((tile_rows, head_count, query_group_width, HEAD_SIZE), jnp.float32),
        )
        return (HEAD_SIZE ** (-0.5) * summed).astype(jnp.bfloat16)

    offsets = jnp.arange(query_rows_4d.shape[0] // tile_rows, dtype=jnp.int32) * tile_rows
    return lax.map(query_one_block, offsets).reshape(query_rows_4d.shape)


def key_grads(
    key_rows_3d,
    value_rows_3d,
    key_pos,
    key_doc,
    query_rows_4d,
    output_gradient_4d,
    query_pos,
    query_doc,
    log_total,
    row_delta,
    tile_rows,
):
    head_count = key_rows_3d.shape[1]
    query_tiles = query_rows_4d.shape[0] // tile_rows

    def key_one_block(offset):
        key_block = window_of(key_rows_3d, offset, tile_rows, 0)
        value_block = window_of(value_rows_3d, offset, tile_rows, 0)
        key_place = window_of(key_pos, offset, tile_rows, 0)
        key_label = window_of(key_doc, offset, tile_rows, 0)

        def key_gather_terms(number, carried):
            first = number * tile_rows
            query_block = window_of(query_rows_4d, first, tile_rows, 0)
            grad_block = window_of(output_gradient_4d, first, tile_rows, 0)
            query_place = window_of(query_pos, first, tile_rows, 0)
            query_label = window_of(query_doc, first, tile_rows, 0)
            total_block = window_of(log_total, first, tile_rows, 2)
            delta_block = window_of(row_delta, first, tile_rows, 2)

            def key_update(running):
                key_sum, value_sum = running
                scores = masked_scores(
                    query_block, key_block, query_label, key_label, query_place, key_place
                )
                prob = jnp.exp(scores - total_block[..., None])
                grad_weights = jnp.einsum(
                    "qhgd,khd->hgqk", grad_block, value_block, preferred_element_type=jnp.float32
                )
                grad_scores = (prob * (grad_weights - delta_block[..., None])).astype(jnp.bfloat16)
                weights = prob.astype(jnp.bfloat16)
                key_sum = key_sum + jnp.einsum(
                    "hgqk,qhgd->khd", grad_scores, query_block, preferred_element_type=jnp.float32
                )
                value_sum = value_sum + jnp.einsum(
                    "hgqk,qhgd->khd", weights, grad_block, preferred_element_type=jnp.float32
                )
                return (key_sum, value_sum)

            return lax.cond(
                touches(query_label, key_label, query_place, key_place),
                key_update,
                lambda unchanged: unchanged,
                carried,
            )

        zeros_sum = jnp.zeros((tile_rows, head_count, HEAD_SIZE), jnp.float32)
        return lax.fori_loop(0, query_tiles, key_gather_terms, (zeros_sum, zeros_sum))

    offsets = jnp.arange(key_rows_3d.shape[0] // tile_rows, dtype=jnp.int32) * tile_rows
    key_sum, value_sum = lax.map(key_one_block, offsets)
    return (key_sum.reshape(key_rows_3d.shape), value_sum.reshape(key_rows_3d.shape))


def shards(queries, keys, values, output_gradient, doc_lengths):
    query_rows, key_rows, value_rows, grad_rows = (
        lax.all_to_all(queries, "head", split_axis=1, concat_axis=0, tiled=True),
        lax.all_to_all(keys, "head", split_axis=1, concat_axis=0, tiled=True),
        lax.all_to_all(values, "head", split_axis=1, concat_axis=0, tiled=True),
        lax.all_to_all(output_gradient, "head", split_axis=1, concat_axis=0, tiled=True),
    )
    length = query_rows.shape[0]
    kv_count = key_rows.shape[1] // HEAD_SIZE
    query_group_width = query_rows.shape[1] // (kv_count * HEAD_SIZE)
    tile_rows = min(512, length)
    query_rows_4d = query_rows.reshape(length, kv_count, query_group_width, HEAD_SIZE)
    output_gradient_4d = grad_rows.reshape(length, kv_count, query_group_width, HEAD_SIZE)
    key_rows_3d = key_rows.reshape(length, kv_count, HEAD_SIZE)
    value_rows_3d = value_rows.reshape(length, kv_count, HEAD_SIZE)
    doc_ends = jnp.cumsum(doc_lengths)
    anchor = lax.axis_index("ctx") * length
    own_pos = anchor + jnp.arange(length, dtype=jnp.int32)
    own_doc = document_ids(doc_ends, own_pos)
    earlier = [
        from_behind((key_rows_3d, value_rows_3d), "ctx", REACH - number) for number in range(REACH)
    ]
    span_keys = jnp.concatenate([member[0] for member in earlier] + [key_rows_3d], axis=0)
    span_values = jnp.concatenate([member[1] for member in earlier] + [value_rows_3d], axis=0)
    span_pos = anchor - REACH * length + jnp.arange((REACH + 1) * length, dtype=jnp.int32)
    span_doc = document_ids(doc_ends, span_pos)
    log_total, attended = attend(
        query_rows_4d, own_pos, own_doc, span_keys, span_values, span_pos, span_doc, tile_rows
    )
    out_piece = lax.all_to_all(
        attended.reshape(length, -1), "head", split_axis=0, concat_axis=1, tiled=True
    )
    row_delta = jnp.moveaxis(
        jnp.sum(output_gradient_4d.astype(jnp.float32) * attended.astype(jnp.float32), axis=-1),
        0,
        2,
    )
    grad_query = query_grads(
        query_rows_4d,
        output_gradient_4d,
        own_pos,
        own_doc,
        log_total,
        row_delta,
        span_keys,
        span_values,
        span_pos,
        span_doc,
        tile_rows,
    )
    later_rows = [
        from_behind((query_rows_4d, output_gradient_4d), "ctx", -number)
        for number in range(1, REACH + 1)
    ]
    later_stats = [
        from_behind((log_total, row_delta), "ctx", -number) for number in range(1, REACH + 1)
    ]
    reach_queries = jnp.concatenate([query_rows_4d] + [member[0] for member in later_rows], axis=0)
    reach_grads = jnp.concatenate(
        [output_gradient_4d] + [member[1] for member in later_rows], axis=0
    )
    reach_total = jnp.concatenate([log_total] + [member[0] for member in later_stats], axis=2)
    reach_delta = jnp.concatenate([row_delta] + [member[1] for member in later_stats], axis=2)
    reach_pos = anchor + jnp.arange((REACH + 1) * length, dtype=jnp.int32)
    reach_doc = document_ids(doc_ends, reach_pos)
    key_sum, value_sum = key_grads(
        key_rows_3d,
        value_rows_3d,
        own_pos,
        own_doc,
        reach_queries,
        reach_grads,
        reach_pos,
        reach_doc,
        reach_total,
        reach_delta,
        tile_rows,
    )
    grad_key_rows = (HEAD_SIZE ** (-0.5) * key_sum).astype(jnp.bfloat16).reshape(length, -1)
    grad_value_rows = value_sum.astype(jnp.bfloat16).reshape(length, -1)
    query_piece, key_piece, value_piece = (
        lax.all_to_all(
            grad_query.reshape(length, -1), "head", split_axis=0, concat_axis=1, tiled=True
        ),
        lax.all_to_all(grad_key_rows, "head", split_axis=0, concat_axis=1, tiled=True),
        lax.all_to_all(grad_value_rows, "head", split_axis=0, concat_axis=1, tiled=True),
    )
    return (out_piece, query_piece, key_piece, value_piece)


def solution(mesh):
    return jax.shard_map(
        shards,
        mesh=mesh,
        in_specs=(
            P(("ctx", "head"), None),
            P(("ctx", "head"), None),
            P(("ctx", "head"), None),
            P(("ctx", "head"), None),
            P(),
        ),
        out_specs=(
            P(("ctx", "head"), None),
            P(("ctx", "head"), None),
            P(("ctx", "head"), None),
            P(("ctx", "head"), None),
        ),
        check_vma=False,
    )
```

profile of v0, /device:TPU:4, one launch (start us, length us, event | category | flops | bytes accessed | tf_op | source)
XLA Modules:
  0.0 1001.0 jit_solution(2355702779607357193)
XLA Ops:
  12.5 10.3 %all-to-all-done.2 = bf16[128,8,128]{2,0,1:T(8,128)(2,1)} async-done(((bf16[128,8,128]{2,0,1:T(8,128)(2,1)}), bf16[128,8,128]{2,0,1:T(8,128)(2,1)}, u32[]{:S(2)}, u32[]{:S(2)}) %all-to-all-start.2) | async-done | bytes 262176 | tf_op jit(solution)/shard_map/all_to_all | solution.py:255
  42.2 24.8 %all-to-all-done.4 = bf16[128,8,512]{0,2,1:T(8,128)(2,1)S(1)} async-done(((bf16[128,8,512]{0,2,1:T(8,128)(2,1)}), bf16[128,8,512]{0,2,1:T(8,128)(2,1)S(1)}, u32[]{:S(2)}, u32[]{:S(2)}) %all-to-all-start.4) | async-done | bytes 1048608 | tf_op jit(solution)/shard_map/all_to_all | solution.py:256
  106.9 351.3 %while.103 = (s32[]{:T(128)}, f32[2,1,4,512]{3,2,1,0:T(4,128)S(1)}, bf16[2,512,1,4,128]{1,4,3,2,0:T(8,128)(2,1)}, s32[2]{0:T(128)}, s32[1024]{0:T(1024)}, /*inde...) while((s32[]{:T(128)}, f32[2,1,4,512]{3,2,1,0:T(4,128)S(1)}, ...), condition=%wide.region_14.15_spmd.clone, body=%wide.region_3.14_spmd.clone.sunk | while | flops 561253376 | bytes 124648104 | solution.py:117
  111.8 80.8 %while.108 = (s32[]{:T(128)}, f32[6,1,4,512,512]{3,4,2,1,0:T(8,128)}, s32[3072]{0:T(1024)S(1)}, s32[512]{0:T(512)S(1)}, s32[3072]{0:T(1024)S(1)}, /*index=5*/s32...) while((s32[]{:T(128)}, ...), condition=%wide.region_7.7_spmd, body=%wide.region_4.6_spmd.sunk | while | flops 271319040 | bytes 13779781 | solution.py:77
  192.7 9.2 reduce_max.11
  201.8 10.0 %exponential_reduce_fusion.2 = f32[4,512]{1,0:T(4,128)S(1)} fusion(f32[6,1,4,512,512]{3,4,2,1,0:T(8,128)} %get-tuple-element.2253, f32[4,512]{1,0:T(4,128)S(1)} %reduce_max.11), kind=kLoop, calls=%fused_computation.81.clone.1 | loop fusion | flops 12580864 | bytes 25182208 | tf_op jit(solution)/shard_map/while/body/eval_jaxpr/reduce_sum | solution.py:88
  211.9 25.0 %copy.154 = f32[6,1,4,512,512]{4,3,2,1,0:T(8,128)} copy(f32[6,1,4,512,512]{3,4,2,1,0:T(8,128)} %get-tuple-element.2253) | data formatting | bytes 50331648 | tf_op jit(solution)/shard_map/while/body/eval_jaxpr/while | solution.py:108
  237.0 50.6 %while.109 = (s32[]{:T(128)}, f32[512,1,4,128]{0,3,2,1:T(8,128)S(1)}, s32[3072]{0:T(1024)S(1)}, s32[512]{0:T(512)S(1)}, s32[3072]{0:T(1024)S(1)}, /*index=5*/s32...) while((s32[]{:T(128)}, ...), condition=%wide.region_13.13_spmd, body=%wide.region_10.12_spmd.sunk | while | flops 270794752 | bytes 6439783 | solution.py:108
  293.4 79.2 %while.108 = (s32[]{:T(128)}, f32[6,1,4,512,512]{3,4,2,1,0:T(8,128)}, s32[3072]{0:T(1024)S(1)}, s32[512]{0:T(512)S(1)}, s32[3072]{0:T(1024)S(1)}, /*index=5*/s32...) while((s32[]{:T(128)}, ...), condition=%wide.region_7.7_spmd, body=%wide.region_4.6_spmd.sunk | while | flops 271319040 | bytes 13779781 | solution.py:77
  381.7 10.0 %exponential_reduce_fusion.2 = f32[4,512]{1,0:T(4,128)S(1)} fusion(f32[6,1,4,512,512]{3,4,2,1,0:T(8,128)} %get-tuple-element.2253, f32[4,512]{1,0:T(4,128)S(1)} %reduce_max.11), kind=kLoop, calls=%fused_computation.81.clone.1 | loop fusion | flops 12580864 | bytes 25182208 | tf_op jit(solution)/shard_map/while/body/eval_jaxpr/reduce_sum | solution.py:88
  391.8 25.0 %copy.154 = f32[6,1,4,512,512]{4,3,2,1,0:T(8,128)} copy(f32[6,1,4,512,512]{3,4,2,1,0:T(8,128)} %get-tuple-element.2253) | data formatting | bytes 50331648 | tf_op jit(solution)/shard_map/while/body/eval_jaxpr/while | solution.py:108
  416.9 40.4 %while.109 = (s32[]{:T(128)}, f32[512,1,4,128]{0,3,2,1:T(8,128)S(1)}, s32[3072]{0:T(1024)S(1)}, s32[512]{0:T(512)S(1)}, s32[3072]{0:T(1024)S(1)}, /*index=5*/s32...) while((s32[]{:T(128)}, ...), condition=%wide.region_13.13_spmd, body=%wide.region_10.12_spmd.sunk | while | flops 270794752 | bytes 6439783 | solution.py:108
  480.9 13.9 %collective-permute-done.4 = bf16[1024,1,4,128]{0,3,2,1:T(8,128)(2,1)} collective-permute-done((bf16[1024,1,4,128]{0,3,2,1:T(8,128)(2,1)}, bf16[1024,1,4,128]{0,3,2,1:T(8,128)(2,1)}, u32[]{:S(2)}, u32[]{:S(2)}) %collective-permute-start.4) | collective-permute-done | bytes 1048608 | tf_op jit(solution)/shard_map/ppermute | solution.py:13
  494.7 16.6 %collective-permute-done.5 = bf16[1024,1,4,128]{0,3,2,1:T(8,128)(2,1)} collective-permute-done((bf16[1024,1,4,128]{0,3,2,1:T(8,128)(2,1)}, bf16[1024,1,4,128]{0,3,2,1:T(8,128)(2,1)}, u32[]{:S(2)}, u32[]{:S(2)}) %collective-permute-start.5) | collective-permute-done | bytes 1048608 | tf_op jit(solution)/shard_map/ppermute | solution.py:13
  517.9 257.3 %while.107 = (s32[]{:T(128)}, f32[2,512,1,128]{3,1,0,2:T(8,128)}, bf16[2,512,1,128]{3,1,0,2:T(8,128)(2,1)}, s32[2]{0:T(128)}, s32[1024]{0:T(1024)}, /*index=5*/s...) while((s32[]{:T(128)}, f32[2,512,1,128]{3,1,0,2:T(8,128)}, ...), condition=%wide.region_28.29_spmd.clone, body=%wide.region_23.28_spmd.clone.sunk | while | flops 1085148160 | bytes 19627356 | solution.py:247
  527.5 122.7 %while.111 = (s32[]{:T(128)}, f32[512,1,128]{0,2,1:T(8,128)}, f32[512,1,128]{0,2,1:T(8,128)}, s32[512]{0:T(512)}, s32[3072]{0:T(1024)}, /*index=5*/s32[512]{0:T(...) while((s32[]{:T(128)}, f32[512,1,128]{0,2,1:T(8,128)}, ...), condition=%wide.region_27.27_spmd, body=%wide.region_24.26_spmd.sunk | while | flops 1085145088 | bytes 16852928 | solution.py:244
  536.0 14.3 %conditional.8 = ((f32[512,1,128]{0,2,1:T(8,128)}, f32[512,1,128]{0,2,1:T(8,128)})) conditional(s32[]{:T(128)} %bitcast.288, (f32[512,1,128]{0,2,1:T(8,128)}, f32[512,1,128]{0,2,1:T(8,128)}) %tuple.266, (bf16[3072,1,4,128]{3,0,2,1:T(8,128)(2,1)S(1)}, s32[]{:T(128)}, s32[512]{0:T(512)S(1)}, s32[512]{0:T(512)}, s32[512]{0:T(512)}, ...), branch_computations={%region_25.24_spmd, %region_26.25_spmd} | conditional | flops 1085145088 | bytes 16844320 | solution.py:236
  558.8 14.3 %conditional.8 = ((f32[512,1,128]{0,2,1:T(8,128)}, f32[512,1,128]{0,2,1:T(8,128)})) conditional(s32[]{:T(128)} %bitcast.288, (f32[512,1,128]{0,2,1:T(8,128)}, f32[512,1,128]{0,2,1:T(8,128)}) %tuple.266, (bf16[3072,1,4,128]{3,0,2,1:T(8,128)(2,1)S(1)}, s32[]{:T(128)}, s32[512]{0:T(512)S(1)}, s32[512]{0:T(512)}, s32[512]{0:T(512)}, ...), branch_computations={%region_25.24_spmd, %region_26.25_spmd} | conditional | flops 1085145088 | bytes 16844320 | solution.py:236
  581.6 14.3 %conditional.8 = ((f32[512,1,128]{0,2,1:T(8,128)}, f32[512,1,128]{0,2,1:T(8,128)})) conditional(s32[]{:T(128)} %bitcast.288, (f32[512,1,128]{0,2,1:T(8,128)}, f32[512,1,128]{0,2,1:T(8,128)}) %tuple.266, (bf16[3072,1,4,128]{3,0,2,1:T(8,128)(2,1)S(1)}, s32[]{:T(128)}, s32[512]{0:T(512)S(1)}, s32[512]{0:T(512)}, s32[512]{0:T(512)}, ...), branch_computations={%region_25.24_spmd, %region_26.25_spmd} | conditional | flops 1085145088 | bytes 16844320 | solution.py:236
  604.4 14.3 %conditional.8 = ((f32[512,1,128]{0,2,1:T(8,128)}, f32[512,1,128]{0,2,1:T(8,128)})) conditional(s32[]{:T(128)} %bitcast.288, (f32[512,1,128]{0,2,1:T(8,128)}, f32[512,1,128]{0,2,1:T(8,128)}) %tuple.266, (bf16[3072,1,4,128]{3,0,2,1:T(8,128)(2,1)S(1)}, s32[]{:T(128)}, s32[512]{0:T(512)S(1)}, s32[512]{0:T(512)}, s32[512]{0:T(512)}, ...), branch_computations={%region_25.24_spmd, %region_26.25_spmd} | conditional | flops 1085145088 | bytes 16844320 | solution.py:236
  627.3 14.3 %conditional.8 = ((f32[512,1,128]{0,2,1:T(8,128)}, f32[512,1,128]{0,2,1:T(8,128)})) conditional(s32[]{:T(128)} %bitcast.288, (f32[512,1,128]{0,2,1:T(8,128)}, f32[512,1,128]{0,2,1:T(8,128)}) %tuple.266, (bf16[3072,1,4,128]{3,0,2,1:T(8,128)(2,1)S(1)}, s32[]{:T(128)}, s32[512]{0:T(512)S(1)}, s32[512]{0:T(512)}, s32[512]{0:T(512)}, ...), branch_computations={%region_25.24_spmd, %region_26.25_spmd} | conditional | flops 1085145088 | bytes 16844320 | solution.py:236
  663.3 108.4 %while.111 = (s32[]{:T(128)}, f32[512,1,128]{0,2,1:T(8,128)}, f32[512,1,128]{0,2,1:T(8,128)}, s32[512]{0:T(512)}, s32[3072]{0:T(1024)}, /*index=5*/s32[512]{0:T(...) while((s32[]{:T(128)}, f32[512,1,128]{0,2,1:T(8,128)}, ...), condition=%wide.region_27.27_spmd, body=%wide.region_24.26_spmd.sunk | while | flops 1085145088 | bytes 16852928 | solution.py:244
  680.3 14.3 %conditional.8 = ((f32[512,1,128]{0,2,1:T(8,128)}, f32[512,1,128]{0,2,1:T(8,128)})) conditional(s32[]{:T(128)} %bitcast.288, (f32[512,1,128]{0,2,1:T(8,128)}, f32[512,1,128]{0,2,1:T(8,128)}) %tuple.266, (bf16[3072,1,4,128]{3,0,2,1:T(8,128)(2,1)S(1)}, s32[]{:T(128)}, s32[512]{0:T(512)S(1)}, s32[512]{0:T(512)}, s32[512]{0:T(512)}, ...), branch_computations={%region_25.24_spmd, %region_26.25_spmd} | conditional | flops 1085145088 | bytes 16844320 | solution.py:236
  703.1 14.3 %conditional.8 = ((f32[512,1,128]{0,2,1:T(8,128)}, f32[512,1,128]{0,2,1:T(8,128)})) conditional(s32[]{:T(128)} %bitcast.288, (f32[512,1,128]{0,2,1:T(8,128)}, f32[512,1,128]{0,2,1:T(8,128)}) %tuple.266, (bf16[3072,1,4,128]{3,0,2,1:T(8,128)(2,1)S(1)}, s32[]{:T(128)}, s32[512]{0:T(512)S(1)}, s32[512]{0:T(512)}, s32[512]{0:T(512)}, ...), branch_computations={%region_25.24_spmd, %region_26.25_spmd} | conditional | flops 1085145088 | bytes 16844320 | solution.py:236
  726.0 14.3 %conditional.8 = ((f32[512,1,128]{0,2,1:T(8,128)}, f32[512,1,128]{0,2,1:T(8,128)})) conditional(s32[]{:T(128)} %bitcast.288, (f32[512,1,128]{0,2,1:T(8,128)}, f32[512,1,128]{0,2,1:T(8,128)}) %tuple.266, (bf16[3072,1,4,128]{3,0,2,1:T(8,128)(2,1)S(1)}, s32[]{:T(128)}, s32[512]{0:T(512)S(1)}, s32[512]{0:T(512)}, s32[512]{0:T(512)}, ...), branch_computations={%region_25.24_spmd, %region_26.25_spmd} | conditional | flops 1085145088 | bytes 16844320 | solution.py:236
  748.8 14.3 %conditional.8 = ((f32[512,1,128]{0,2,1:T(8,128)}, f32[512,1,128]{0,2,1:T(8,128)})) conditional(s32[]{:T(128)} %bitcast.288, (f32[512,1,128]{0,2,1:T(8,128)}, f32[512,1,128]{0,2,1:T(8,128)}) %tuple.266, (bf16[3072,1,4,128]{3,0,2,1:T(8,128)(2,1)S(1)}, s32[]{:T(128)}, s32[512]{0:T(512)S(1)}, s32[512]{0:T(512)}, s32[512]{0:T(512)}, ...), branch_computations={%region_25.24_spmd, %region_26.25_spmd} | conditional | flops 1085145088 | bytes 16844320 | solution.py:236
  784.1 10.5 %all-to-all-done.6 = bf16[8,128,128]{2,1,0:T(8,128)(2,1)S(1)} async-done(((bf16[8,128,128]{2,1,0:T(8,128)(2,1)}), bf16[8,128,128]{2,1,0:T(8,128)(2,1)S(1)}, u32[]{:S(2)}, u32[]{:S(2)}) %all-to-all-start.6) | async-done | bytes 262176 | tf_op jit(solution)/shard_map/all_to_all | solution.py:335
  798.7 150.5 %while.105 = (s32[]{:T(128)}, bf16[2,512,1,4,128]{4,3,1,0,2:T(4,128)(2,1)S(1)}, s32[2]{0:T(128)}, s32[1024]{0:T(1024)}, s32[1024]{0:T(1024)}, /*index=5*/bf16[10...) while((s32[]{:T(128)}, ...), condition=%wide.region_21.22_spmd.clone, body=%wide.region_16.21_spmd.clone.sunk | while | flops 813173760 | bytes 20404508 | solution.py:183
  807.1 78.1 %while.110 = (s32[]{:T(128)}, f32[512,1,4,128]{0,3,2,1:T(8,128)S(1)}, s32[3072]{0:T(1024)S(1)}, s32[512]{0:T(512)S(1)}, s32[3072]{0:T(1024)}, /*index=5*/s32[512...) while((s32[]{:T(128)}, ...), condition=%wide.region_20.20_spmd, body=%wide.region_17.19_spmd.sunk | while | flops 812646400 | bytes 12486537 | solution.py:174
  894.3 54.1 %while.110 = (s32[]{:T(128)}, f32[512,1,4,128]{0,3,2,1:T(8,128)S(1)}, s32[3072]{0:T(1024)S(1)}, s32[512]{0:T(512)S(1)}, s32[3072]{0:T(1024)}, /*index=5*/s32[512...) while((s32[]{:T(128)}, ...), condition=%wide.region_20.20_spmd, body=%wide.region_17.19_spmd.sunk | while | flops 812646400 | bytes 12486537 | solution.py:174
  959.6 17.0 %all-to-all-done.5 = bf16[8,128,512]{2,1,0:T(8,128)(2,1)S(1)} async-done(((bf16[8,128,512]{2,1,0:T(8,128)(2,1)}), bf16[8,128,512]{2,1,0:T(8,128)(2,1)S(1)}, u32[]{:S(2)}, u32[]{:S(2)}) %all-to-all-start.5) | async-done | bytes 1048608 | tf_op jit(solution)/shard_map/all_to_all | solution.py:332
  985.1 13.9 %all-to-all-done.3 = bf16[8,128,512]{2,1,0:T(8,128)(2,1)S(1)} async-done(((bf16[8,128,512]{2,1,0:T(8,128)(2,1)}), bf16[8,128,512]{2,1,0:T(8,128)(2,1)S(1)}, u32[]{:S(2)}, u32[]{:S(2)}) %all-to-all-start.3) | async-done | bytes 1048608 | tf_op jit(solution)/shard_map/all_to_all | solution.py:280
  (560 shorter events, 734.2 us)
Async XLA Ops:
  0.6 40.2 %copy-start.7 = (bf16[128,4096]{1,0:T(8,128)(2,1)S(1)}, bf16[128,4096]{1,0:T(8,128)(2,1)}, u32[]{:S(2)}) copy-start(bf16[128,4096]{1,0:T(8,128)(2,1)} %param.27) | copy-start | bytes 3145732
  2.3 20.4 %all-to-all-start.2 = ((bf16[128,8,128]{2,0,1:T(8,128)(2,1)}), bf16[128,8,128]{2,0,1:T(8,128)(2,1)}, u32[]{:S(2)}, u32[]{:S(2)}) async-start(bf16[128,8,128]{2,0,1:T(8,128)(2,1)} %copy_bitcast_fusion), calls=%async_computation.2 | async-start | bytes 524288 | tf_op jit(solution)/shard_map/all_to_all | solution.py:255
  22.8 14.5 %all-to-all-start.1 = ((bf16[128,8,128]{2,0,1:T(8,128)(2,1)}), bf16[128,8,128]{2,0,1:T(8,128)(2,1)}, u32[]{:S(2)}, u32[]{:S(2)}) async-start(bf16[128,8,128]{2,0,1:T(8,128)(2,1)} %copy_bitcast_fusion.1), calls=%async_computation.1 | async-start | bytes 524288 | tf_op jit(solution)/shard_map/all_to_all | solution.py:254
  26.8 43.7 %copy-start.13 = (s32[64]{0:T(128)S(1)}, s32[64]{0:T(128)}, u32[]{:S(2)}) copy-start(s32[64]{0:T(128)} %param.31) | copy-start | bytes 772
  37.3 29.7 %all-to-all-start.4 = ((bf16[128,8,512]{0,2,1:T(8,128)(2,1)}), bf16[128,8,512]{0,2,1:T(8,128)(2,1)S(1)}, u32[]{:S(2)}, u32[]{:S(2)}) async-start(bf16[128,8,512]{0,2,1:T(8,128)(2,1)} %bitcast.67), calls=%async_computation.4 | async-start | bytes 2097152 | tf_op jit(solution)/shard_map/all_to_all | solution.py:256
  67.0 36.3 %all-to-all-start = ((bf16[128,8,512]{0,2,1:T(8,128)(2,1)}), bf16[128,8,512]{0,2,1:T(8,128)(2,1)S(1)}, u32[]{:S(2)}, u32[]{:S(2)}) async-start(bf16[128,8,512]{0,2,1:T(8,128)(2,1)} %bitcast.55), calls=%async_computation | async-start | bytes 2097152 | tf_op jit(solution)/shard_map/all_to_all | solution.py:253
  73.7 12.2 %collective-permute-start.2 = (bf16[1024,1,128]{2,0,1:T(8,128)(2,1)}, bf16[1024,1,128]{2,0,1:T(8,128)(2,1)S(1)}, u32[]{:S(2)}, u32[]{:S(2)}) collective-permute-start(bf16[1024,1,128]{2,0,1:T(8,128)(2,1)} %bitcast.61), channel_id=1, source_target_pairs={{0,16},{8,24},{16,32},{24,40},{32,48},{40,56},{48,64},{56,72},{64,... | collective-permute-start | bytes 786440 | tf_op jit(solution)/shard_map/ppermute | solution.py:13
  76.8 9.2 collective-permute-start.3
  79.3 10.8 %collective-permute-start = (bf16[1024,1,128]{2,0,1:T(8,128)(2,1)}, bf16[1024,1,128]{2,0,1:T(8,128)(2,1)}, u32[]{:S(2)}, u32[]{:S(2)}) collective-permute-start(bf16[1024,1,128]{2,0,1:T(8,128)(2,1)} %bitcast.58), channel_id=1, source_target_pairs={{0,16},{8,24},{16,32},{24,40},{32,48},{40,56},{48,64},{56,72},{64,... | collective-permute-start | bytes 786440 | tf_op jit(solution)/shard_map/ppermute | solution.py:13
  82.7 10.8 %collective-permute-start.1 = (bf16[1024,1,128]{2,0,1:T(8,128)(2,1)}, bf16[1024,1,128]{2,0,1:T(8,128)(2,1)}, u32[]{:S(2)}, u32[]{:S(2)}) collective-permute-start(bf16[1024,1,128]{2,0,1:T(8,128)(2,1)} %bitcast.58), channel_id=1, source_target_pairs={{0,8},{8,16},{16,24},{24,32},{32,40},{40,48},{48,56},{56,64},{64,7... | collective-permute-start | bytes 786440 | tf_op jit(solution)/shard_map/ppermute | solution.py:13
  98.7 377.4 %collective-permute-start.8 = (bf16[1024,1,4,128]{0,3,2,1:T(8,128)(2,1)}, bf16[1024,1,4,128]{0,3,2,1:T(8,128)(2,1)}, u32[]{:S(2)}, u32[]{:S(2)}) collective-permute-start(bf16[1024,1,4,128]{0,3,2,1:T(8,128)(2,1)} %reshape.362), channel_id=1, source_target_pairs={{8,0},{16,8},{24,16},{32,24},{40,32},{48,40},{56,48},{64,56},{72,6... | collective-permute-start | bytes 3145736 | tf_op jit(solution)/shard_map/ppermute | solution.py:13
  100.6 375.5 %collective-permute-start.9 = (bf16[1024,1,4,128]{0,3,2,1:T(8,128)(2,1)}, bf16[1024,1,4,128]{0,3,2,1:T(8,128)(2,1)}, u32[]{:S(2)}, u32[]{:S(2)}) collective-permute-start(bf16[1024,1,4,128]{0,3,2,1:T(8,128)(2,1)} %reshape.362), channel_id=1, source_target_pairs={{16,0},{24,8},{32,16},{40,24},{48,32},{56,40},{64,48},{72,56},{80,... | collective-permute-start | bytes 3145736 | tf_op jit(solution)/shard_map/ppermute | solution.py:13
  458.2 4.1 copy-start.2
  458.2 4.1 copy-start.3
  458.2 4.1 copy-start.6
  458.2 17.2 %copy-start.11 = (f32[2,1,4,512]{3,2,1,0:T(4,128)}, f32[2,1,4,512]{3,2,1,0:T(4,128)S(1)}, u32[]{:S(2)}) copy-start(f32[2,1,4,512]{3,2,1,0:T(4,128)S(1)} %get-tuple-element.1216) | copy-start | bytes 49156
  460.4 7.8 copy-start.12
  462.3 18.6 %copy-start.10 = (f32[1024,4]{0,1:T(4,128)}, f32[1024,4]{0,1:T(4,128)S(1)}, u32[]{:S(2)}) copy-start(f32[1024,4]{0,1:T(4,128)S(1)} %multiply_reduce_fusion) | copy-start | bytes 49156
  462.3 6.5 collective-permute-start.10
  464.3 6.4 collective-permute-start.11
  466.3 6.4 collective-permute-start.6
  468.8 6.6 collective-permute-start.7
  470.7 24.0 %collective-permute-start.4 = (bf16[1024,1,4,128]{0,3,2,1:T(8,128)(2,1)}, bf16[1024,1,4,128]{0,3,2,1:T(8,128)(2,1)}, u32[]{:S(2)}, u32[]{:S(2)}) collective-permute-start(bf16[1024,1,4,128]{0,3,2,1:T(8,128)(2,1)} %reshape.358), channel_id=1, source_target_pairs={{8,0},{16,8},{24,16},{32,24},{40,32},{48,40},{56,48},{64,56},{72,6... | collective-permute-start | bytes 3145736 | tf_op jit(solution)/shard_map/ppermute | solution.py:13
  472.7 38.6 %collective-permute-start.5 = (bf16[1024,1,4,128]{0,3,2,1:T(8,128)(2,1)}, bf16[1024,1,4,128]{0,3,2,1:T(8,128)(2,1)}, u32[]{:S(2)}, u32[]{:S(2)}) collective-permute-start(bf16[1024,1,4,128]{0,3,2,1:T(8,128)(2,1)} %reshape.358), channel_id=1, source_target_pairs={{16,0},{24,8},{32,16},{40,24},{48,32},{56,40},{64,48},{72,56},{80,... | collective-permute-start | bytes 3145736 | tf_op jit(solution)/shard_map/ppermute | solution.py:13
  777.0 17.6 %all-to-all-start.6 = ((bf16[8,128,128]{2,1,0:T(8,128)(2,1)}), bf16[8,128,128]{2,1,0:T(8,128)(2,1)S(1)}, u32[]{:S(2)}, u32[]{:S(2)}) async-start(bf16[8,128,128]{2,1,0:T(8,128)(2,1)} %bitcast.75), calls=%async_computation.6 | async-start | bytes 524288 | tf_op jit(solution)/shard_map/all_to_all | solution.py:335
  794.6 4.1 copy-start.8
  794.6 155.8 %all-to-all-start.7 = ((bf16[8,128,128]{2,1,0:T(8,128)(2,1)}), bf16[8,128,128]{2,1,0:T(8,128)(2,1)}, u32[]{:S(2)}, u32[]{:S(2)}) async-start(bf16[8,128,128]{2,1,0:T(8,128)(2,1)} %bitcast.307), calls=%async_computation.7 | async-start | bytes 524288 | tf_op jit(solution)/shard_map/all_to_all | solution.py:336
  949.1 8.5 copy-start.4
  950.4 29.7 %copy-start.9 = (bf16[8,128,128]{2,1,0:T(8,128)(2,1)S(1)}, bf16[8,128,128]{2,1,0:T(8,128)(2,1)}, u32[]{:S(2)}) copy-start(bf16[8,128,128]{2,1,0:T(8,128)(2,1)} %copy-done.8) | copy-start | bytes 786436
  950.4 26.2 %all-to-all-start.5 = ((bf16[8,128,512]{2,1,0:T(8,128)(2,1)}), bf16[8,128,512]{2,1,0:T(8,128)(2,1)S(1)}, u32[]{:S(2)}, u32[]{:S(2)}) async-start(bf16[8,128,512]{2,1,0:T(8,128)(2,1)} %all_to_all.116), calls=%async_computation.5 | async-start | bytes 2097152 | tf_op jit(solution)/shard_map/all_to_all | solution.py:332
  976.5 22.4 %all-to-all-start.3 = ((bf16[8,128,512]{2,1,0:T(8,128)(2,1)}), bf16[8,128,512]{2,1,0:T(8,128)(2,1)S(1)}, u32[]{:S(2)}, u32[]{:S(2)}) async-start(bf16[8,128,512]{2,1,0:T(8,128)(2,1)} %all_to_all.109), calls=%async_computation.3 | async-start | bytes 2097152 | tf_op jit(solution)/shard_map/all_to_all | solution.py:280
  983.1 17.8 %copy-start.1 = (bf16[128,1024]{1,0:T(8,128)(2,1)S(1)}, bf16[128,1024]{1,0:T(8,128)(2,1)}, u32[]{:S(2)}) copy-start(bf16[128,1024]{1,0:T(8,128)(2,1)} %param.29) | copy-start | bytes 786436
  (2 other events, 4.1 us)
where the time goes:
time: 1010 us; the launch traced here: 1000 us
  local copies, waits for them, and re-layouts  339 us (34%)
  matrix products  205 us (20%)
  loops' own time  194 us (19%)
  waiting for transfers between devices  120 us (12%)
  other arithmetic  72.4 us (7%)
  starting transfers between devices  69.6 us (7%)
    dot_general x23, matrix products, masked_scores(): jnp.einsum('qhgd,khd->hgqk', query_block, key_block, preferred_element_ty...  68.8 us
    dynamic_update_slice x12, local copies, waits for them, and re-layouts, score_tile(): return lax.dynamic_update_index_in_dim(stored, tile_scores, number, 0)  55.6 us
    dynamic_slice x120, local copies, waits for them, and re-layouts, window_of(): return lax.dynamic_slice_in_dim(array, offset, length, reduce_axis)  53.8 us
    while x2, local copies, waits for them, and re-layouts, attend_one_block(): lax.fori_loop(0, key_tiles, gather_out, jnp.zeros((tile_rows, head_count,...  50 us
    another operation x2, loops' own time, attend_one_block(): lax.fori_loop(0, key_tiles, score_tile, jnp.full((key_tiles, head_count,...  46.3 us
    another operation x2, loops' own time, key_one_block(): lax.fori_loop(0, query_tiles, key_gather_terms, (zeros_sum, zeros_sum))  45.6 us
    another operation x2, loops' own time, query_one_block(): lax.fori_loop(0, key_tiles, query_gather_terms, jnp.zeros((tile_rows, hea...  44.9 us
    dot_general x9, matrix products, key_update(): jnp.einsum('hgqk,qhgd->khd', grad_scores, query_block, preferred_element_...  44.8 us
  transfers between devices with their start and end apart: 20, of which 10 were waited for; matrix products, arithmetic and copies ran while one was open for 39% of the time, Pallas kernels for 0%

commit v1 on v0

v1 whole, which is shorter than its diff:
```python
import math

import jax
import jax.numpy as jnp
from jax import lax
from jax.experimental import pallas as pl
from jax.experimental.pallas import tpu as pltpu
from jax.sharding import PartitionSpec as P

MESH = pl.DeviceIdType.MESH
D = 128
G = 4
B = 128
PEERS = 8
RING = 8
REACH = 2
SLOTS = PEERS + REACH
CHUNKS = 4
TILE = 256
PAD = 128
KEYS = SLOTS * RING * B
SCALE = D ** (-0.5)
LOG2E = math.log2(math.e)
BF16 = jnp.bfloat16
F32 = jnp.float32


def wrap(a, n):
    return lax.rem(a, n)


def place():
    ctx = lax.axis_index("ctx")
    z = lax.axis_index("head")
    group = lax.div(ctx, PEERS)
    return ctx, z, group, ctx - group * PEERS


def enter(devices):
    barrier = pltpu.get_barrier_semaphore()
    for device in devices:
        pl.semaphore_signal(barrier, inc=1, device_id=device, device_id_type=MESH)
    pl.semaphore_wait(barrier, len(devices))


def neighbours(ctx, z, group, me):
    peers = [(group * PEERS + wrap(me + d, PEERS), z) for d in range(1, PEERS)]
    right, left = (ctx, wrap(z + 1, RING)), (ctx, wrap(z + RING - 1, RING))
    groups = lax.axis_size("ctx") // PEERS
    above = (wrap(group + 1, groups) * PEERS + me, z)
    below = (wrap(group + groups - 1, groups) * PEERS + me, z)
    return peers, right, left, above, below


def remote(src, dst, send, recv, device):
    return pltpu.make_async_remote_copy(
        src_ref=src, dst_ref=dst, send_sem=send, recv_sem=recv, device_id=device, device_id_type=MESH
    )


def gather_kernel(
    q_ref, k_ref, v_ref, g_ref, qh_ref, gh_ref, kv_ref,
    kv_send, kv_recv, row_send, row_recv, ring_send, ring_recv, halo_send, halo_recv, own_sem,
):
    ctx, z, group, me = place()
    peers, right, left, above, below = neighbours(ctx, z, group, me)
    enter(peers + [right, left, above, below])

    def lanes(head, width):
        return pl.ds(pl.multiple_of(head * width, width), width)

    own = [
        pltpu.make_async_copy(k_ref.at[:, lanes(me, D)], kv_ref.at[0, REACH + me, z], own_sem.at[0]),
        pltpu.make_async_copy(v_ref.at[:, lanes(me, D)], kv_ref.at[1, REACH + me, z], own_sem.at[1]),
        pltpu.make_async_copy(q_ref.at[:, lanes(me, G * D)], qh_ref.at[me], own_sem.at[2]),
        pltpu.make_async_copy(g_ref.at[:, lanes(me, G * D)], gh_ref.at[me], own_sem.at[3]),
    ]
    kv_copies, row_copies = [], []
    for d in range(1, PEERS):
        head = wrap(me + d, PEERS)
        for part, ref in enumerate((k_ref, v_ref)):
            kv_copies.append(
                remote(
                    ref.at[:, lanes(head, D)], kv_ref.at[part, REACH + me, z],
                    kv_send.at[part, d - 1], kv_recv.at[part, d - 1], peers[d - 1],
                )
            )
        for part, (ref, out) in enumerate(((q_ref, qh_ref), (g_ref, gh_ref))):
            row_copies.append(
                remote(
                    ref.at[:, lanes(head, G * D)], out.at[me],
                    row_send.at[part, d - 1], row_recv.at[part, d - 1], peers[d - 1],
                )
            )
    for copy in own[:2] + kv_copies:
        copy.start()
    for copy in own[:2]:
        copy.wait()
    for copy in kv_copies:
        copy.wait()

    def piece(chunk, offset):
        return kv_ref.at[:, pl.ds(REACH + 2 * chunk, 2), wrap(z + offset + RING, RING)]

    ring = {}
    for way, device in ((0, right), (1, left)):
        for step in range(4):
            for chunk in range(CHUNKS):
                if step == 3 and (chunk < 2) != (way == 0):
                    continue
                block = piece(chunk, -step if way == 0 else step)
                ring[way, step, chunk] = remote(
                    block, block, ring_send.at[way, step, chunk], ring_recv.at[way, step, chunk], device
                )
    halo = []

    def send_halo(offset):
        number = len(halo)
        where = wrap(z + offset + RING, RING)
        copy = remote(
            kv_ref.at[:, pl.ds(PEERS, REACH), where], kv_ref.at[:, pl.ds(0, REACH), where],
            halo_send.at[number], halo_recv.at[number], above,
        )
        copy.start()
        halo.append(copy)

    order = (3, 0, 2, 1)
    for chunk in order:
        for way in (0, 1):
            ring[way, 0, chunk].start()
    send_halo(0)
    for copy in own[2:] + row_copies:
        copy.start()
    for step in range(4):
        for chunk in order:
            for way in (0, 1):
                if (way, step, chunk) not in ring:
                    continue
                ring[way, step, chunk].wait_recv()
                if (way, step + 1, chunk) in ring:
                    ring[way, step + 1, chunk].start()
                if chunk == 3:
                    send_halo(-(step + 1) if way == 0 else step + 1)
    for copy in own[2:] + row_copies:
        copy.wait()
    for copy in ring.values():
        copy.wait_send()
    for copy in halo:
        copy.wait()


def gather(queries, keys, values, gradient):
    anywhere = pl.BlockSpec(memory_space=pl.ANY)
    dma = pltpu.SemaphoreType.DMA
    return pl.pallas_call(
        gather_kernel,
        out_shape=(
            jax.ShapeDtypeStruct((PEERS, B, G * D), BF16),
            jax.ShapeDtypeStruct((PEERS, B, G * D), BF16),
            jax.ShapeDtypeStruct((2, SLOTS, RING, B, D), BF16),
        ),
        in_specs=[anywhere] * 4,
        out_specs=[anywhere] * 3,
        scratch_shapes=[
            dma((2, PEERS - 1)), dma((2, PEERS - 1)), dma((2, PEERS - 1)), dma((2, PEERS - 1)),
            dma((2, 4, CHUNKS)), dma((2, 4, CHUNKS)), dma((RING,)), dma((RING,)), dma((4,)),
        ],
        compiler_params=pltpu.CompilerParams(collective_id=0, has_side_effects=True),
        name="gather",
    )(queries, keys, values, gradient)


def attention_kernel(
    length_ref, q_ref, g_ref, kv_ref, att_ref, dq_ref, dkv_ref,
    kv, dk, dv, score, acc, starts, stage, bounds, load_sem, store_sem,
):
    step = pl.program_id(0)
    _, z, group, _ = place()
    base = (group * PEERS - REACH) * (RING * B)
    first = base + REACH * RING * B + z * B

    def fetch(part, slot):
        rows = RING * B
        return pltpu.make_async_copy(
            kv_ref.at[part, slot], kv.at[part, pl.ds(PAD + slot * rows, rows)], load_sem.at[part, slot]
        )

    @pl.when(step == 0)
    def _():
        for slot in range(SLOTS):
            for part in range(2):
                fetch(part, slot).start()
        kv[:, :PAD, :] = jnp.zeros((2, PAD, D), BF16)
        dk[...] = jnp.zeros_like(dk)
        dv[...] = jnp.zeros_like(dv)
        shape = (PEERS, B)
        positions = (
            first
            + lax.broadcasted_iota(jnp.int32, shape, 0) * (RING * B)
            + lax.broadcasted_iota(jnp.int32, shape, 1)
        )

        def one_doc(number, carried):
            start, vector, low, high = carried
            vector = jnp.where(positions >= start, start, vector)
            low = [jnp.where(first + i * (RING * B) >= start, start, low[i]) for i in range(PEERS)]
            high = [
                jnp.where(first + i * (RING * B) + B - 1 >= start, start, high[i]) for i in range(PEERS)
            ]
            return start + length_ref[number], vector, low, high

        zero = jnp.int32(0)
        _, vector, low, high = lax.fori_loop(
            0, length_ref.shape[0], one_doc,
            (zero, jnp.zeros(shape, jnp.int32), [zero] * PEERS, [zero] * PEERS),
        )
        starts[...] = vector
        for i in range(PEERS):
            bounds[0, i] = low[i]
            bounds[1, i] = high[i]
        for slot in range(SLOTS):
            for part in range(2):
                fetch(part, slot).wait()

    def heads(ref):
        return jnp.concatenate([ref[0, :, h * D : (h + 1) * D] for h in range(G)], axis=0)

    origin = first + step * (RING * B) - base + PAD
    end = origin + B
    low = bounds[0, step] - base + PAD
    high = bounds[1, step] - base + PAD
    tiles = lax.div(end - low + TILE - 1, TILE)
    queries, gradient = heads(q_ref), heads(g_ref)
    start_row = starts[pl.ds(step, 1), :] - base + PAD
    start_row = jnp.concatenate([start_row] * G, axis=1)
    token_row = origin + lax.rem(lax.broadcasted_iota(jnp.int32, (1, G * B), 1), B)

    def rows_of(tile):
        return pl.ds(pl.multiple_of(end - (tile + 1) * TILE, 128), TILE)

    def fold(x, op):
        return op(x.reshape(TILE // 8, 8, G * B), axis=0)

    def first_pass(tile, top):
        s = lax.dot_general(
            kv[0, rows_of(tile), :], queries, (((1,), (1,)), ((), ())), preferred_element_type=F32
        )
        at = end - (tile + 1) * TILE

        def masked(s):
            row = at + lax.broadcasted_iota(jnp.int32, s.shape, 0)
            return jnp.where((row >= start_row) & (row <= token_row), s, -1e30)

        s = lax.cond((tile == 0) | (at < high), masked, lambda s: s, s)
        score[tile] = s
        return jnp.maximum(top, fold(s, jnp.max))

    top = lax.fori_loop(0, tiles, first_pass, jnp.full((8, G * B), -1e30, F32))
    top = jnp.max(top, axis=0, keepdims=True)

    acc[...] = jnp.zeros_like(acc)

    def second_pass(tile, total):
        e = jnp.exp2((score[tile] - top) * (SCALE * LOG2E))
        score[tile] = e
        acc[...] += lax.dot_general(
            kv[1, rows_of(tile), :], e.astype(BF16), (((0,), (0,)), ((), ())), preferred_element_type=F32
        )
        return total + fold(e, jnp.sum)

    total = lax.fori_loop(0, tiles, second_pass, jnp.zeros((8, G * B), F32))
    inverse = 1.0 / jnp.sum(total, axis=0, keepdims=True)
    attended = (acc[...] * inverse).astype(BF16).astype(F32)
    turned = jnp.concatenate([gradient[h * B : (h + 1) * B].astype(F32).T for h in range(G)], axis=1)
    delta = jnp.sum(attended * turned, axis=0, keepdims=True)
    for h in range(G):
        att_ref[0, :, h * D : (h + 1) * D] = attended[:, h * B : (h + 1) * B].T.astype(BF16)

    acc[...] = jnp.zeros_like(acc)

    def third_pass(tile, carried):
        rows = rows_of(tile)
        dp = lax.dot_general(
            kv[1, rows, :], gradient, (((1,), (1,)), ((), ())), preferred_element_type=F32
        )
        p = score[tile] * inverse
        ds = (p * (dp - delta)).astype(BF16)
        dv[rows, :] += jnp.dot(p.astype(BF16), gradient, preferred_element_type=F32)
        dk[rows, :] += jnp.dot(ds, queries, preferred_element_type=F32)
        acc[...] += lax.dot_general(
            kv[0, rows, :], ds, (((0,), (0,)), ((), ())), preferred_element_type=F32
        )
        return carried

    lax.fori_loop(0, tiles, third_pass, 0)
    for h in range(G):
        dq_ref[0, :, h * D : (h + 1) * D] = (SCALE * acc[:, h * B : (h + 1) * B].T).astype(BF16)

    def put(part, slot):
        return pltpu.make_async_copy(stage.at[part, slot], dkv_ref.at[part, slot], store_sem.at[part, slot])

    def finish(slot):
        rows = RING * B
        at = pl.ds(pl.multiple_of(PAD + slot * rows, 128), rows)
        stage[0, slot] = (SCALE * dk[at, :]).astype(BF16)
        stage[1, slot] = dv[at, :].astype(BF16)
        put(0, slot).start()
        put(1, slot).start()

    finish(step)

    @pl.when(step == PEERS - 1)
    def _():
        for slot in range(PEERS, SLOTS):
            finish(slot)
        for slot in range(SLOTS):
            put(0, slot).wait()
            put(1, slot).wait()


def attention(doc_lengths, queries, gradient, kv):
    block = pl.BlockSpec((1, B, G * D), lambda i, *_: (i, 0, 0))
    anywhere = pl.BlockSpec(memory_space=pl.ANY)
    shard = RING * B
    return pl.pallas_call(
        attention_kernel,
        grid_spec=pltpu.PrefetchScalarGridSpec(
            num_scalar_prefetch=1,
            grid=(PEERS,),
            in_specs=[block, block, anywhere],
            out_specs=[block, block, anywhere],
            scratch_shapes=[
                pltpu.VMEM((2, PAD + KEYS, D), BF16),
                pltpu.VMEM((PAD + KEYS, D), F32),
                pltpu.VMEM((PAD + KEYS, D), F32),
                pltpu.VMEM((9, TILE, G * B), F32),
                pltpu.VMEM((D, G * B), F32),
                pltpu.VMEM((PEERS, B), jnp.int32),
                pltpu.VMEM((2, SLOTS, shard, D), BF16),
                pltpu.SMEM((2, PEERS), jnp.int32),
                pltpu.SemaphoreType.DMA((2, SLOTS)),
                pltpu.SemaphoreType.DMA((2, SLOTS)),
            ],
        ),
        out_shape=(
            jax.ShapeDtypeStruct((PEERS, B, G * D), BF16),
            jax.ShapeDtypeStruct((PEERS, B, G * D), BF16),
            jax.ShapeDtypeStruct((2, SLOTS, shard, D), BF16),
        ),
        compiler_params=pltpu.CompilerParams(vmem_limit_bytes=50 * 2**20),
        name="attention",
    )(doc_lengths, queries, gradient, kv.reshape(2, SLOTS, shard, D))


def scatter_kernel(
    att_ref, dq_ref, part_ref, att_out, dq_out, dk_out, dv_out,
    buf, fresh, halo_buf, done,
    row_send, row_recv, ring_send, ring_recv, halo_send, halo_recv, kv_send, kv_recv, own_sem,
):
    ctx, z, group, me = place()
    peers, right, left, above, below = neighbours(ctx, z, group, me)
    enter(peers + [right, left, above, below])

    def lanes(head, width):
        return pl.ds(pl.multiple_of(head * width, width), width)

    halo = {}
    for offset in (4, 3, 5, 2, 6, 1, 7, 0):
        halo[offset] = remote(
            part_ref.at[:, pl.ds(0, REACH), wrap(z + offset, RING)], halo_buf.at[offset],
            halo_send.at[offset], halo_recv.at[offset], below,
        )

    def piece(chunk, offset):
        return part_ref.at[:, pl.ds(REACH + 2 * chunk, 2), wrap(z + offset, RING)]

    def part(chunk, offset):
        value = piece(chunk, offset)[...].astype(F32)
        if chunk == CHUNKS - 1:
            value = value + halo_buf[offset].astype(F32)
        return value

    hops_of = lambda way, chunk: 4 if (chunk < 2) == (way == 0) else 3
    offset_of = lambda way, hops: hops if way == 0 else (RING - hops) % RING
    ring = {}
    for way, device in ((0, right), (1, left)):
        for chunk in range(CHUNKS):
            for hops in range(1, hops_of(way, chunk) + 1):
                if hops < hops_of(way, chunk):
                    source = buf.at[way, hops, chunk]
                elif chunk == CHUNKS - 1:
                    source = fresh.at[way]
                else:
                    source = piece(chunk, offset_of(way, hops))
                ring[way, hops, chunk] = remote(
                    source, buf.at[way, hops - 1, chunk],
                    ring_send.at[way, hops - 1, chunk], ring_recv.at[way, hops - 1, chunk], device,
                )
    own, rows = [], []
    for number, (ref, out) in enumerate(((att_ref, att_out), (dq_ref, dq_out))):
        own.append(pltpu.make_async_copy(ref.at[me], out.at[:, lanes(me, G * D)], own_sem.at[number]))
        for d in range(1, PEERS):
            rows.append(
                remote(
                    ref.at[wrap(me + d, PEERS)], out.at[:, lanes(me, G * D)],
                    row_send.at[number, d - 1], row_recv.at[number, d - 1], peers[d - 1],
                )
            )

    order = (0, 2, 1, 3)
    for turn in range(4):
        for chunk in order:
            for way in (0, 1):
                hops = hops_of(way, chunk) - turn
                if hops < 1:
                    continue
                offset = offset_of(way, hops)
                if chunk == CHUNKS - 1:
                    halo[offset].wait_recv()
                if turn:
                    ring[way, hops + 1, chunk].wait_recv()
                    mine = buf.at[way, hops, chunk]
                    mine[...] = (mine[...].astype(F32) + part(chunk, offset)).astype(BF16)
                elif chunk == CHUNKS - 1:
                    fresh[way] = part(chunk, offset).astype(BF16)
                ring[way, hops, chunk].start()
            if turn == 0 and chunk == order[0]:
                for copy in halo.values():
                    copy.start()
        if turn == 0:
            for copy in own + rows:
                copy.start()
    halo[0].wait_recv()
    last = []
    for chunk in order:
        for way in (0, 1):
            ring[way, 1, chunk].wait_recv()
        value = part(chunk, 0) + buf[0, 0, chunk].astype(F32) + buf[1, 0, chunk].astype(F32)
        done[:, 2 * chunk : 2 * chunk + 2] = value.astype(BF16)
    for number, out in enumerate((dk_out, dv_out)):
        own.append(
            pltpu.make_async_copy(done.at[number, me], out.at[:, lanes(me, D)], own_sem.at[2 + number])
        )
        own[-1].start()
        for d in range(1, PEERS):
            last.append(
                remote(
                    done.at[number, wrap(me + d, PEERS)], out.at[:, lanes(me, D)],
                    kv_send.at[number, d - 1], kv_recv.at[number, d - 1], peers[d - 1],
                )
            )
            last[-1].start()
    for copy in own + rows + last:
        copy.wait()
    for copy in ring.values():
        copy.wait_send()
    for copy in halo.values():
        copy.wait_send()


def scatter(attended, grad_queries, parts):
    anywhere = pl.BlockSpec(memory_space=pl.ANY)
    dma = pltpu.SemaphoreType.DMA
    return pl.pallas_call(
        scatter_kernel,
        out_shape=(
            jax.ShapeDtypeStruct((B, PEERS * G * D), BF16),
            jax.ShapeDtypeStruct((B, PEERS * G * D), BF16),
            jax.ShapeDtypeStruct((B, PEERS * D), BF16),
            jax.ShapeDtypeStruct((B, PEERS * D), BF16),
        ),
        in_specs=[anywhere, anywhere, pl.BlockSpec(memory_space=pltpu.VMEM)],
        out_specs=[anywhere] * 4,
        scratch_shapes=[
            pltpu.VMEM((2, 4, CHUNKS, 2, 2, B, D), BF16),
            pltpu.VMEM((2, 2, 2, B, D), BF16),
            pltpu.VMEM((RING, 2, REACH, B, D), BF16),
            pltpu.VMEM((2, PEERS, B, D), BF16),
            dma((2, PEERS - 1)), dma((2, PEERS - 1)), dma((2, 4, CHUNKS)), dma((2, 4, CHUNKS)),
            dma((RING,)), dma((RING,)), dma((2, PEERS - 1)), dma((2, PEERS - 1)), dma((4,)),
        ],
        compiler_params=pltpu.CompilerParams(
            collective_id=1, has_side_effects=True, vmem_limit_bytes=40 * 2**20
        ),
        name="scatter",
    )(attended, grad_queries, parts)


def shards(queries, keys, values, output_gradient, doc_lengths):
    query_rows, grad_rows, kv = gather(queries, keys, values, output_gradient)
    attended, grad_queries, parts = attention(doc_lengths, query_rows, grad_rows, kv)
    return scatter(attended, grad_queries, parts.reshape(2, SLOTS, RING, B, D))


def solution(mesh):
    rows = P(("ctx", "head"), None)
    return jax.shard_map(
        shards, mesh=mesh, in_specs=(rows, rows, rows, rows, P()), out_specs=(rows,) * 4, check_vma=False
    )
```

time: 1010 us -> 170 us (0.17)
  the two profiles are of different devices: /device:TPU:4 before, /device:TPU:1 now
where the time goes in v1:
time: 170 us; the launch traced here: 168 us
  Pallas kernels  160 us (94%)
  local copies, waits for them, and re-layouts  7.7 us (5%)
    pallas_call x1, Pallas kernels, scatter(): pl.pallas_call(scatter_kernel, out_shape=(jax.ShapeDtypeStruct((B, PEERS...  72.7 us
    pallas_call x1, Pallas kernels, gather(): pl.pallas_call(gather_kernel, out_shape=(jax.ShapeDtypeStruct((PEERS, B,...  61 us
    pallas_call x1, Pallas kernels, attention(): pl.pallas_call(attention_kernel, grid_spec=pltpu.PrefetchScalarGridSpec(n...  26 us
    unnamed x10, local copies, waits for them, and re-layouts  7.7 us

profile of v1, /device:TPU:1, one launch (start us, length us, event | category | flops | bytes accessed | tf_op | source)
XLA Modules:
  0.0 168.1 jit_solution(8435742576296766140)
XLA Ops:
  0.6 61.0 %gather.1 = (bf16[8,128,512]{2,1,0:T(8,128)(2,1)}, bf16[8,128,512]{2,1,0:T(8,128)(2,1)}, bf16[2,10,8,128,128]{4,3,2,1,0:T(8,128)(2,1)}) custom-call(bf16[128,4096]{1,0:T(8,128)(2,1)} %q_ref.1, bf16[128,1024]{1,0:T(8,128)(2,1)} %k_ref.1, bf16[128,1024]{1,0:T(8,128)(2,1)} %v_ref.1, bf16[128,4096]{1,0:T(8,128)(2,1)} %g_ref.1), custom_call_target="tpu_custom_call" | custom-call | tf_op jit(solution)/shard_map/gather/pallas_call | solution.py:155
  61.6 0.0 copy-start.1
  61.6 1.2 copy-done.1
  62.9 0.0 copy-start.2
  62.9 0.7 copy-done.2
  63.5 26.0 %attention.1 = (bf16[8,128,512]{2,1,0:T(8,128)(2,1)S(1)}, bf16[8,128,512]{2,1,0:T(8,128)(2,1)S(1)}, bf16[2,10,1024,128]{3,2,1,0:T(8,128)(2,1)}) custom-call(s32[64]{0:T(128)S(1)} %copy-done.2, bf16[8,128,512]{2,1,0:T(8,128)(2,1)S(1)} %copy-done.1, bf16[8,128,512]{2,1,0:T(8,128)(2,1)} %get-tuple-element.11.g_ref, bf16[2,10,1024,128]{3,2,1,0:T(8,128)(2,1)} %bitcast.3), custom_call_target="tpu_custom_call" | custom-call | tf_op jit(solution)/shard_map/attention/pallas_call | solution.py:325
  89.5 0.0 copy-start
  89.5 2.5 %copy-done = bf16[2,10,1024,128]{3,2,1,0:T(8,128)(2,1)S(1)} copy-done((bf16[2,10,1024,128]{3,2,1,0:T(8,128)(2,1)S(1)}, bf16[2,10,1024,128]{3,2,1,0:T(8,128)(2,1)}, u32[]{:S(2)}) %copy-start) | copy-done | bytes 5242904
  92.0 72.7 %scatter.1 = (bf16[128,4096]{1,0:T(8,128)(2,1)S(1)}, bf16[128,4096]{1,0:T(8,128)(2,1)S(1)}, bf16[128,1024]{1,0:T(8,128)(2,1)S(1)}, bf16[128,1024]{1,0:T(8,128)(2,1)S(1)}) custom-call(bf16[8,128,512]{2,1,0:T(8,128)(2,1)S(1)} %get-tuple-element.13.att_ref, bf16[8,128,512]{2,1,0:T(8,128)(2,1)S(1)} %get-tuple-element.14.dq_ref, ...), custom_call_target="tpu_custom_call" | custom-call | tf_op jit(solution)/shard_map/scatter/pallas_call | solution.py:464
  164.7 1.0 copy.13
  165.7 1.0 copy.14
  166.6 0.7 copy.15
  167.4 0.7 copy.16
Async XLA Ops:
  61.6 1.2 copy-start.1
  62.9 0.7 copy-start.2
  89.5 2.5 %copy-start = (bf16[2,10,1024,128]{3,2,1,0:T(8,128)(2,1)S(1)}, bf16[2,10,1024,128]{3,2,1,0:T(8,128)(2,1)}, u32[]{:S(2)}) copy-start(bf16[2,10,1024,128]{3,2,1,0:T(8,128)(2,1)} %get-tuple-element.15) | copy-start | bytes 15728644

commit v2 on v1

--- a/solution.py
+++ b/solution.py
@@ -17,6 +17,7 @@
 SLOTS = PEERS + REACH
 CHUNKS = 4
 TILE = 256
+SIZES = (4, 2, 1)
 PAD = 128
 KEYS = SLOTS * RING * B
 SCALE = D ** (-0.5)
@@ -201,74 +202,89 @@
         )
 
         def one_doc(number, carried):
-            start, vector, low, high = carried
+            start, vector, low = carried
             vector = jnp.where(positions >= start, start, vector)
             low = [jnp.where(first + i * (RING * B) >= start, start, low[i]) for i in range(PEERS)]
-            high = [
-                jnp.where(first + i * (RING * B) + B - 1 >= start, start, high[i]) for i in range(PEERS)
-            ]
-            return start + length_ref[number], vector, low, high
+            return start + length_ref[number], vector, low
 
         zero = jnp.int32(0)
-        _, vector, low, high = lax.fori_loop(
+        _, vector, low = lax.fori_loop(
             0, length_ref.shape[0], one_doc,
-            (zero, jnp.zeros(shape, jnp.int32), [zero] * PEERS, [zero] * PEERS),
+            (zero, jnp.zeros(shape, jnp.int32), [zero] * PEERS),
         )
         starts[...] = vector
         for i in range(PEERS):
-            bounds[0, i] = low[i]
-            bounds[1, i] = high[i]
-        for slot in range(SLOTS):
+            bounds[i] = low[i]
+        for slot in range(REACH):
             for part in range(2):
                 fetch(part, slot).wait()
 
+    for part in range(2):
+        fetch(part, REACH + step).wait()
+
     def heads(ref):
         return jnp.concatenate([ref[0, :, h * D : (h + 1) * D] for h in range(G)], axis=0)
 
     origin = first + step * (RING * B) - base + PAD
     end = origin + B
-    low = bounds[0, step] - base + PAD
-    high = bounds[1, step] - base + PAD
+    low = bounds[step] - base + PAD
     tiles = lax.div(end - low + TILE - 1, TILE)
     queries, gradient = heads(q_ref), heads(g_ref)
     start_row = starts[pl.ds(step, 1), :] - base + PAD
     start_row = jnp.concatenate([start_row] * G, axis=1)
-    token_row = origin + lax.rem(lax.broadcasted_iota(jnp.int32, (1, G * B), 1), B)
-
-    def rows_of(tile):
-        return pl.ds(pl.multiple_of(end - (tile + 1) * TILE, 128), TILE)
+    token_row = lax.rem(lax.broadcasted_iota(jnp.int32, (1, G * B), 1), B)
+
+    def sweep(body, carried):
+        loops = lax.div(tiles, SIZES[0])
+        carried = lax.fori_loop(
+            0, loops, lambda i, c: body(i * (SIZES[0] * TILE), SIZES[0] * TILE, c), carried
+        )
+        left, done = tiles - loops * SIZES[0], loops * SIZES[0]
+        for size in SIZES[1:]:
+            carried = lax.cond(
+                left >= size, lambda c: body(done * TILE, size * TILE, c), lambda c: c, carried
+            )
+            taken = jnp.where(left >= size, size, 0)
+            left, done = left - taken, done + taken
+        return carried
+
+    def rows_of(ahead, size):
+        return pl.ds(pl.multiple_of(end - ahead - size, 128), size)
+
+    def stored(ahead, size):
+        return pl.ds(pl.multiple_of(ahead, TILE), size)
 
     def fold(x, op):
-        return op(x.reshape(TILE // 8, 8, G * B), axis=0)
-
-    def first_pass(tile, top):
+        return op(x.reshape(x.shape[0] // 8, 8, G * B), axis=0)
+
+    def first_pass(ahead, size, top):
         s = lax.dot_general(
-            kv[0, rows_of(tile), :], queries, (((1,), (1,)), ((), ())), preferred_element_type=F32
-        )
-        at = end - (tile + 1) * TILE
-
-        def masked(s):
-            row = at + lax.broadcasted_iota(jnp.int32, s.shape, 0)
-            return jnp.where((row >= start_row) & (row <= token_row), s, -1e30)
-
-        s = lax.cond((tile == 0) | (at < high), masked, lambda s: s, s)
-        score[tile] = s
+            kv[0, rows_of(ahead, size), :], queries, (((1,), (1,)), ((), ())), preferred_element_type=F32
+        )
+        row = lax.broadcasted_iota(jnp.int32, s.shape, 0)
+        s = jnp.where(row >= start_row - (end - ahead - size), s, -1e30)
+        late = s[size - B :]
+        row = lax.broadcasted_iota(jnp.int32, late.shape, 0)
+        late = jnp.where(row <= token_row + ahead, late, -1e30)
+        s = jnp.concatenate([s[: size - B], late], axis=0)
+        score[stored(ahead, size), :] = s
         return jnp.maximum(top, fold(s, jnp.max))
 
-    top = lax.fori_loop(0, tiles, first_pass, jnp.full((8, G * B), -1e30, F32))
+    top = sweep(first_pass, jnp.full((8, G * B), -1e30, F32))
     top = jnp.max(top, axis=0, keepdims=True)
 
     acc[...] = jnp.zeros_like(acc)
 
-    def second_pass(tile, total):
-        e = jnp.exp2((score[tile] - top) * (SCALE * LOG2E))
-        score[tile] = e
+    def second_pass(ahead, size, total):
+        e = jnp.exp2((score[stored(ahead, size), :] - top) * (SCALE * LOG2E))
+        score[stored(ahead, size), :] = e
         acc[...] += lax.dot_general(
-            kv[1, rows_of(tile), :], e.astype(BF16), (((0,), (0,)), ((), ())), preferred_element_type=F32
+            kv[1, rows_of(ahead, size), :], e.astype(BF16), (((0,), (0,)), ((), ())),
+            preferred_element_type=F32,
         )
         return total + fold(e, jnp.sum)
 
-    total = lax.fori_loop(0, tiles, second_pass, jnp.zeros((8, G * B), F32))
+    total = sweep(second_pass, jnp.zeros((8, G * B), F32))
     inverse = 1.0 / jnp.sum(total, axis=0, keepdims=True)
     attended = (acc[...] * inverse).astype(BF16).astype(F32)
     turned = jnp.concatenate([gradient[h * B : (h + 1) * B].astype(F32).T for h in range(G)], axis=1)
@@ -278,12 +294,12 @@
 
     acc[...] = jnp.zeros_like(acc)
 
-    def third_pass(tile, carried):
-        rows = rows_of(tile)
+    def third_pass(ahead, size, carried):
+        rows = rows_of(ahead, size)
         dp = lax.dot_general(
             kv[1, rows, :], gradient, (((1,), (1,)), ((), ())), preferred_element_type=F32
         )
-        p = score[tile] * inverse
+        p = score[stored(ahead, size), :] * inverse
         ds = (p * (dp - delta)).astype(BF16)
         dv[rows, :] += jnp.dot(p.astype(BF16), gradient, preferred_element_type=F32)
         dk[rows, :] += jnp.dot(ds, queries, preferred_element_type=F32)
@@ -292,7 +308,7 @@
         )
         return carried
 
-    lax.fori_loop(0, tiles, third_pass, 0)
+    sweep(third_pass, 0)
     for h in range(G):
         dq_ref[0, :, h * D : (h + 1) * D] = (SCALE * acc[:, h * B : (h + 1) * B].T).astype(BF16)
 
@@ -333,11 +349,11 @@
                 pltpu.VMEM((2, PAD + KEYS, D), BF16),
                 pltpu.VMEM((PAD + KEYS, D), F32),
                 pltpu.VMEM((PAD + KEYS, D), F32),
-                pltpu.VMEM((9, TILE, G * B), F32),
+                pltpu.VMEM((9 * TILE, G * B), F32),
                 pltpu.VMEM((D, G * B), F32),
                 pltpu.VMEM((PEERS, B), jnp.int32),
                 pltpu.VMEM((2, SLOTS, shard, D), BF16),
-                pltpu.SMEM((2, PEERS), jnp.int32),
+                pltpu.SMEM((PEERS,), jnp.int32),
                 pltpu.SemaphoreType.DMA((2, SLOTS)),
                 pltpu.SemaphoreType.DMA((2, SLOTS)),
             ],

time: 170 us -> 151 us (0.89); the launches traced: 168 us -> 151 us
  Pallas kernels: 160 us -> 143 us
    pallas_call x1, Pallas kernels: 72.7 us -> 60.7 us  [scatter(): pl.pallas_call(scatter_kernel, out_shape=(jax.ShapeDtypeStruct((B, PEERS...]
    pallas_call x1, Pallas kernels: 26 us -> 21.2 us  [attention(): pl.pallas_call(attention_kernel, grid_spec=pltpu.PrefetchScalarGridSpec(n...]
where the time goes in v2:
time: 151 us
  Pallas kernels  143 us (95%)
  local copies, waits for them, and re-layouts  7.7 us (5%)
    pallas_call x1, Pallas kernels, gather(): pl.pallas_call(gather_kernel, out_shape=(jax.ShapeDtypeStruct((PEERS, B,...  61 us
    pallas_call x1, Pallas kernels, scatter(): pl.pallas_call(scatter_kernel, out_shape=(jax.ShapeDtypeStruct((B, PEERS...  60.7 us
    pallas_call x1, Pallas kernels, attention(): pl.pallas_call(attention_kernel, grid_spec=pltpu.PrefetchScalarGridSpec(n...  21.2 us
    unnamed x10, local copies, waits for them, and re-layouts  7.7 us

profile of v2, /device:TPU:1, one launch (start us, length us, event | category | flops | bytes accessed | tf_op | source)
XLA Modules:
  0.0 151.3 jit_solution(4084250277872570382)
XLA Ops:
  0.6 61.0 %gather.1 = (bf16[8,128,512]{2,1,0:T(8,128)(2,1)}, bf16[8,128,512]{2,1,0:T(8,128)(2,1)}, bf16[2,10,8,128,128]{4,3,2,1,0:T(8,128)(2,1)}) custom-call(bf16[128,4096]{1,0:T(8,128)(2,1)} %q_ref.1, bf16[128,1024]{1,0:T(8,128)(2,1)} %k_ref.1, bf16[128,1024]{1,0:T(8,128)(2,1)} %v_ref.1, bf16[128,4096]{1,0:T(8,128)(2,1)} %g_ref.1), custom_call_target="tpu_custom_call" | custom-call | tf_op jit(solution)/shard_map/gather/pallas_call | solution.py:156
  61.6 0.0 copy-start.1
  61.6 1.2 copy-done.1
  62.9 0.0 copy-start.2
  62.9 0.7 copy-done.2
  63.5 21.2 %attention.1 = (bf16[8,128,512]{2,1,0:T(8,128)(2,1)S(1)}, bf16[8,128,512]{2,1,0:T(8,128)(2,1)S(1)}, bf16[2,10,1024,128]{3,2,1,0:T(8,128)(2,1)}) custom-call(s32[64]{0:T(128)S(1)} %copy-done.2, bf16[8,128,512]{2,1,0:T(8,128)(2,1)S(1)} %copy-done.1, bf16[8,128,512]{2,1,0:T(8,128)(2,1)} %get-tuple-element.11.g_ref, bf16[2,10,1024,128]{3,2,1,0:T(8,128)(2,1)} %bitcast.3), custom_call_target="tpu_custom_call" | custom-call | tf_op jit(solution)/shard_map/attention/pallas_call | solution.py:341
  84.8 0.0 copy-start
  84.8 2.5 %copy-done = bf16[2,10,1024,128]{3,2,1,0:T(8,128)(2,1)S(1)} copy-done((bf16[2,10,1024,128]{3,2,1,0:T(8,128)(2,1)S(1)}, bf16[2,10,1024,128]{3,2,1,0:T(8,128)(2,1)}, u32[]{:S(2)}) %copy-start) | copy-done | bytes 5242904
  87.2 60.7 %scatter.1 = (bf16[128,4096]{1,0:T(8,128)(2,1)S(1)}, bf16[128,4096]{1,0:T(8,128)(2,1)S(1)}, bf16[128,1024]{1,0:T(8,128)(2,1)S(1)}, bf16[128,1024]{1,0:T(8,128)(2,1)S(1)}) custom-call(bf16[8,128,512]{2,1,0:T(8,128)(2,1)S(1)} %get-tuple-element.13.att_ref, bf16[8,128,512]{2,1,0:T(8,128)(2,1)S(1)} %get-tuple-element.14.dq_ref, ...), custom_call_target="tpu_custom_call" | custom-call | tf_op jit(solution)/shard_map/scatter/pallas_call | solution.py:480
  147.9 1.0 copy.13
  148.9 1.0 copy.14
  149.9 0.7 copy.15
  150.6 0.7 copy.16
Async XLA Ops:
  61.6 1.2 copy-start.1
  62.9 0.7 copy-start.2
  84.8 2.5 %copy-start = (bf16[2,10,1024,128]{3,2,1,0:T(8,128)(2,1)S(1)}, bf16[2,10,1024,128]{3,2,1,0:T(8,128)(2,1)}, u32[]{:S(2)}) copy-start(bf16[2,10,1024,128]{3,2,1,0:T(8,128)(2,1)} %get-tuple-element.15) | copy-start | bytes 15728644

commit v3 on v0

v3 whole, which is shorter than its diff:
```python
import math

import jax
import jax.numpy as jnp
from jax import lax
from jax.experimental import pallas as pl
from jax.experimental.pallas import tpu as pltpu
from jax.sharding import PartitionSpec as P

MESH = pl.DeviceIdType.MESH
D = 128
G = 4
B = 128
PEERS = 8
RING = 8
REACH = 2
SLOTS = PEERS + REACH
CHUNKS = 4
SHARD = RING * B
ROWS = G * B
HOPS = 4
UNSEEN = -1e30
SCALE = D ** (-0.5)
LOG2E = math.log2(math.e)
BF16 = jnp.bfloat16
F32 = jnp.float32


def wrap(a, n):
    return lax.rem(a, n)


def place():
    ctx = lax.axis_index("ctx")
    z = lax.axis_index("head")
    group = lax.div(ctx, PEERS)
    return ctx, z, group, ctx - group * PEERS


def enter(devices):
    barrier = pltpu.get_barrier_semaphore()
    for device in devices:
        pl.semaphore_signal(barrier, inc=1, device_id=device, device_id_type=MESH)
    pl.semaphore_wait(barrier, len(devices))


def neighbours(ctx, z, group, me):
    peers = [(group * PEERS + wrap(me + d, PEERS), z) for d in range(1, PEERS)]
    right, left = (ctx, wrap(z + 1, RING)), (ctx, wrap(z + RING - 1, RING))
    groups = lax.axis_size("ctx") // PEERS
    above = (wrap(group + 1, groups) * PEERS + me, z)
    below = (wrap(group + groups - 1, groups) * PEERS + me, z)
    return peers, right, left, above, below


def remote(src, dst, send, recv, device):
    return pltpu.make_async_remote_copy(
        src_ref=src, dst_ref=dst, send_sem=send, recv_sem=recv, device_id=device, device_id_type=MESH
    )


def kernel(
    length_ref, q_ref, k_ref, v_ref, g_ref, att_out, dq_out, dk_out, dv_out,
    kv, qs, gs, acc, top, total, shift, delta, starts, atts, dqs, sums, mine, buf, halo_buf,
    kv_send, kv_recv, row_send, row_recv, ring_send, ring_recv, halo_send, halo_recv,
    out_send, out_recv, back_send, back_recv, gone_send, gone_recv, last_send, last_recv, own_sem,
):
    ctx, z, group, me = place()
    peers, right, left, above, below = neighbours(ctx, z, group, me)
    base = (group * PEERS - REACH) * SHARD
    enter(peers + [right, left, above, below])

    def lanes(head, width):
        if isinstance(head, int):
            return pl.ds(head * width, width)
        return pl.ds(pl.multiple_of(head * width, width), width)

    def at(offset):
        return wrap(z + offset, RING)

    def exchange(ref, width, target, send, recv, own):
        copies = [pltpu.make_async_copy(ref.at[:, lanes(me, width)], target, own)]
        for d in range(1, PEERS):
            head = wrap(me + d, PEERS)
            copies.append(
                remote(ref.at[:, lanes(head, width)], target, send.at[d - 1], recv.at[d - 1], peers[d - 1])
            )
        return copies

    key_copies = [
        copy
        for part, ref in enumerate((k_ref, v_ref))
        for copy in exchange(
            ref, D, kv.at[part, REACH + me, z], kv_send.at[part], kv_recv.at[part], own_sem.at[part]
        )
    ]
    query_copies = exchange(q_ref, G * D, qs.at[me], row_send.at[0], row_recv.at[0], own_sem.at[2])
    grad_copies = exchange(g_ref, G * D, gs.at[me], row_send.at[1], row_recv.at[1], own_sem.at[3])
    for copy in key_copies:
        copy.start()

    positions = (
        base + REACH * SHARD + z * B
        + lax.broadcasted_iota(jnp.int32, (PEERS, B), 0) * SHARD
        + lax.broadcasted_iota(jnp.int32, (PEERS, B), 1)
    )

    def one_doc(number, carried):
        start, vector = carried
        return start + length_ref[number], jnp.where(positions >= start, start, vector)

    _, vector = lax.fori_loop(
        0, length_ref.shape[0], one_doc, (jnp.int32(0), jnp.zeros((PEERS, B), jnp.int32))
    )
    starts[...] = jnp.concatenate([vector - base] * G, axis=1)
    token = lax.rem(lax.broadcasted_iota(jnp.int32, (1, ROWS), 1), B)

    def ring(way, step, chunk):
        offset = step if way else (RING - step) % RING
        block = kv.at[:, pl.ds(REACH + 2 * chunk, 2), at(offset)]
        return remote(
            block, block, ring_send.at[way, step, chunk], ring_recv.at[way, step, chunk], left if way else right
        )

    def halo(offset):
        return remote(
            kv.at[:, pl.ds(PEERS, REACH), at(offset)], kv.at[:, pl.ds(0, REACH), at(offset)],
            halo_send.at[offset], halo_recv.at[offset], above,
        )

    def arrive(step, turn):
        chunk = CHUNKS - 1 - turn
        for way in (0, 1):
            far = (turn < 2) if way else (turn >= 2)
            if step < HOPS:
                ring(way, step - 1, chunk).wait_recv()
            else:
                pl.when(far)(lambda: ring(way, step - 1, chunk).wait_recv())
            if step < HOPS - 1:
                ring(way, step, chunk).start()
            elif step == HOPS - 1:
                pl.when(far)(lambda: ring(way, step, chunk).start())

        @pl.when(turn == 0)
        def _():
            halo(step).start()
            if step < HOPS:
                halo(RING - step).start()

    def rows(ref, i):
        return jnp.concatenate([ref[i, :, h * D : (h + 1) * D] for h in range(G)], axis=0)

    def keys_of(i, offset):
        if offset == 0:
            return i, 3
        return i + lax.div(z + offset, RING), 2

    def scores(i, offset, queries):
        slot, count = keys_of(i, offset)
        where = at(offset)
        keys = kv[0, pl.ds(slot, count), where].reshape(count * B, D)
        s = lax.dot_general(keys, queries, (((1,), (1,)), ((), ())), preferred_element_type=F32)
        limit = starts[pl.ds(i, 1), :] - (slot * SHARD + where * B)
        row = lax.broadcasted_iota(jnp.int32, (B, ROWS), 0)
        parts = []
        for n in range(count):
            seen = row >= limit - n * SHARD
            if offset == 0 and n == count - 1:
                seen = seen & (row <= token)
            parts.append(jnp.where(seen, s[n * B : (n + 1) * B], UNSEEN))
        return keys, jnp.concatenate(parts, axis=0)

    def values_of(i, offset):
        slot, count = keys_of(i, offset)
        return kv[1, pl.ds(slot, count), at(offset)].reshape(count * B, D)

    def fold(x, op):
        return op(x.reshape(x.shape[0] // 8, 8, ROWS), axis=0)

    def turned_dot(a, b):
        return lax.dot_general(a, b, (((0,), (0,)), ((), ())), preferred_element_type=F32)

    def forward(pair, offset):
        blocks = (2 * pair, 2 * pair + 1)
        found = [scores(i, offset, rows(qs, i))[1] for i in blocks]
        high = [jnp.max(fold(s, jnp.max), axis=0, keepdims=True) for s in found]
        before = [None if offset == 0 else top[pl.ds(i, 1), :] for i in blocks]
        if offset:
            high = [jnp.maximum(a, b) for a, b in zip(high, before)]
        e = [jnp.exp2((s - h) * (SCALE * LOG2E)) for s, h in zip(found, high)]
        out = [turned_dot(values_of(i, offset), x.astype(BF16)) for i, x in zip(blocks, e)]
        count = [fold(x, jnp.sum) for x in e]
        if offset:
            less = [jnp.exp2((b - h) * (SCALE * LOG2E)) for b, h in zip(before, high)]
            out = [acc[i] * f + o for i, f, o in zip(blocks, less, out)]
            count = [total[i] * f + c for i, f, c in zip(blocks, less, count)]
        for i, h, o, c in zip(blocks, high, out, count):
            top[pl.ds(i, 1), :] = h
            acc[i] = o
            total[i] = c

    def four(step, offsets):
        def turn(k, carried):
            if step is not None:
                arrive(step, k)

            @pl.when(k == CHUNKS - 1)
            def _():
                for offset in offsets:
                    halo(offset).wait_recv()

            pair = lax.rem(k + 1, PEERS // 2)
            for offset in offsets:
                forward(pair, offset)
            return carried

        lax.fori_loop(0, CHUNKS, turn, 0)

    for copy in key_copies:
        copy.wait()
    for chunk in reversed(range(CHUNKS)):
        for way in (0, 1):
            ring(way, 0, chunk).start()
    halo(0).start()
    for copy in query_copies:
        copy.start()
    for k in range(CHUNKS):
        arrive(1, k)
    for copy in query_copies:
        copy.wait()
    for copy in grad_copies:
        copy.start()
    four(2, (0, 7, 1))
    four(3, (6, 2))
    four(4, (5, 3))
    four(None, (4,))
    for copy in grad_copies:
        copy.wait()

    def close(i, carried):
        count = jnp.sum(total[i], axis=0, keepdims=True)
        attended = (acc[i] * (1.0 / count)).astype(BF16).astype(F32)
        shift[pl.ds(i, 1), :] = top[pl.ds(i, 1), :] * (SCALE * LOG2E) + jnp.log(count) * LOG2E
        turned = jnp.concatenate([gs[i, :, h * D : (h + 1) * D].astype(F32).T for h in range(G)], axis=1)
        delta[pl.ds(i, 1), :] = jnp.sum(attended * turned, axis=0, keepdims=True)
        for h in range(G):
            atts[i, :, h * D : (h + 1) * D] = attended[:, h * B : (h + 1) * B].T.astype(BF16)
        acc[i] = jnp.zeros((D, ROWS), F32)
        return carried

    lax.fori_loop(0, PEERS, close, 0)

    def give(ref, out, width, send, recv, own):
        copies = [pltpu.make_async_copy(ref.at[me], out.at[:, lanes(me, width)], own)]
        for d in range(1, PEERS):
            copies.append(
                remote(
                    ref.at[wrap(me + d, PEERS)], out.at[:, lanes(me, width)],
                    send.at[d - 1], recv.at[d - 1], peers[d - 1],
                )
            )
        for copy in copies:
            copy.start()
        return copies

    given = give(atts, att_out, G * D, out_send.at[0], out_recv.at[0], own_sem.at[4])

    def backward(pair, offset):
        blocks = (2 * pair, 2 * pair + 1)
        slot, count = keys_of(blocks[0], offset)
        queries, grads = [rows(qs, i) for i in blocks], [rows(gs, i) for i in blocks]
        found = [scores(i, offset, q) for i, q in zip(blocks, queries)]
        dp = [
            lax.dot_general(
                values_of(i, offset), g, (((1,), (1,)), ((), ())), preferred_element_type=F32
            )
            for i, g in zip(blocks, grads)
        ]
        p = [
            jnp.exp2(s * (SCALE * LOG2E) - shift[pl.ds(i, 1), :]) for i, (_, s) in zip(blocks, found)
        ]
        ds = [(a * (b - delta[pl.ds(i, 1), :])).astype(BF16) for i, a, b in zip(blocks, p, dp)]
        dk = [jnp.dot(d, q, preferred_element_type=F32) for d, q in zip(ds, queries)]
        dv = [jnp.dot(a.astype(BF16), g, preferred_element_type=F32) for a, g in zip(p, grads)]
        dq = [turned_dot(keys, d) for (keys, _), d in zip(found, ds)]
        for part, (a, b) in enumerate((dk, dv)):
            middle = a[B:] + b[: (count - 1) * B]
            value = jnp.concatenate([a[:B], middle, b[(count - 1) * B :]], axis=0)
            sums[part, pl.ds(slot, count + 1)] += value.reshape(count + 1, B, D)
        for i, d in zip(blocks, dq):
            acc[i] += d

    def all_backward(offset):
        sums[...] = jnp.zeros_like(sums)

        def one(pair, carried):
            backward(pair, offset)
            return carried

        lax.fori_loop(0, PEERS // 2, one, 0)
        for part, scale in enumerate((SCALE, 1.0)):
            mine[offset, part] = (sums[part] * scale).astype(BF16)
        home(offset).start()

    def home(offset):
        return remote(
            mine.at[offset, :, pl.ds(0, REACH)], halo_buf.at[offset],
            back_send.at[offset], back_recv.at[offset], below,
        )

    def piece(chunk, offset):
        return mine.at[offset, :, pl.ds(REACH + 2 * chunk, 2)]

    def add(target, *others):
        target[...] = sum((ref[...].astype(F32) for ref in others), target[...].astype(F32)).astype(BF16)

    def add_halo(offset):
        home(offset).wait_recv()
        add(piece(CHUNKS - 1, offset), halo_buf.at[offset])

    def most(way, chunk):
        return HOPS if (chunk < 2) == (way == 0) else HOPS - 1

    def message(way, hops, chunk):
        first = hops == most(way, chunk)
        source = piece(chunk, (RING - hops) if way else hops) if first else buf.at[way, hops, chunk]
        return remote(
            source, buf.at[way, hops - 1, chunk],
            gone_send.at[way, hops - 1, chunk], gone_recv.at[way, hops - 1, chunk], left if way else right,
        )

    def post(way, hops, *chunks):
        for chunk in chunks:
            if hops < most(way, chunk):
                message(way, hops + 1, chunk).wait_recv()
                add(buf.at[way, hops, chunk], piece(chunk, (RING - hops) if way else hops))
            message(way, hops, chunk).start()

    all_backward(4)
    post(0, 4, 0, 1)
    post(1, 4, 2)
    all_backward(3)
    post(0, 3, 2)
    add_halo(4)
    post(1, 4, 3)
    all_backward(5)
    add_halo(3)
    post(1, 3, 0, 1)
    post(0, 3, 3, 0, 1)
    post(1, 3, 2)
    all_backward(2)
    add_halo(5)
    post(1, 3, 3)
    post(0, 2, 2)
    all_backward(6)
    add_halo(2)
    post(0, 2, 3)
    all_backward(1)
    add_halo(6)
    post(0, 2, 0, 1)
    post(1, 2, 0, 1, 2)
    all_backward(7)
    add_halo(1)
    post(1, 2, 3)
    post(0, 1, 2)
    all_backward(0)

    def close_query(i, carried):
        for h in range(G):
            dqs[i, :, h * D : (h + 1) * D] = (SCALE * acc[i, :, h * B : (h + 1) * B].T).astype(BF16)
        return carried

    lax.fori_loop(0, PEERS, close_query, 0)
    given += give(dqs, dq_out, G * D, out_send.at[1], out_recv.at[1], own_sem.at[5])
    add_halo(7)
    add_halo(0)
    post(0, 1, 3)
    post(1, 1, 0)
    post(0, 1, 0)
    post(1, 1, 1)
    post(0, 1, 1)
    post(1, 1, 2, 3)

    def last(number, j):
        out = dv_out if number else dk_out
        return remote(
            mine.at[0, number, REACH + j], out.at[:, lanes(me, D)],
            last_send.at[number, j], last_recv.at[number, me], (group * PEERS + j, z),
        )

    for chunk in (0, 2, 1, 3):
        for way in (0, 1):
            message(way, 1, chunk).wait_recv()
        add(piece(chunk, 0), buf.at[0, 0, chunk], buf.at[1, 0, chunk])
        for j in (2 * chunk, 2 * chunk + 1):

            @pl.when(j != me)
            def _():
                last(0, j).start()
                last(1, j).start()

    for number, out in enumerate((dk_out, dv_out)):
        given.append(
            pltpu.make_async_copy(
                mine.at[0, number, REACH + me], out.at[:, lanes(me, D)], own_sem.at[6 + number]
            )
        )
        given[-1].start()
    for copy in given:
        copy.wait()
    for j in range(PEERS):

        @pl.when(j != me)
        def _():
            for number, out in enumerate((dk_out, dv_out)):
                remote(
                    mine.at[0, number, REACH + j], out.at[:, lanes(j, D)],
                    last_send.at[number, j], last_recv.at[number, j], (group * PEERS + j, z),
                ).wait()

    for offset in range(RING):
        halo(offset).wait_send()
        home(offset).wait_send()
    for way in (0, 1):
        for chunk in range(CHUNKS):
            for step in range(most(way, chunk)):
                ring(way, step, chunk).wait_send()
                message(way, step + 1, chunk).wait_send()


def shards(queries, keys, values, output_gradient, doc_lengths):
    anywhere = pl.BlockSpec(memory_space=pltpu.HBM)
    dma = pltpu.SemaphoreType.DMA
    block, message = (B, D), (2, 2, B, D)
    peers, hops = (2, PEERS - 1), (2, HOPS, CHUNKS)
    return pl.pallas_call(
        kernel,
        out_shape=[jax.ShapeDtypeStruct(a.shape, BF16) for a in (queries, queries, keys, values)],
        in_specs=[pl.BlockSpec(memory_space=pltpu.SMEM)] + [anywhere] * 4,
        out_specs=[anywhere] * 4,
        scratch_shapes=[
            pltpu.VMEM((2, SLOTS, RING) + block, BF16),
            pltpu.VMEM((PEERS, B, G * D), BF16),
            pltpu.VMEM((PEERS, B, G * D), BF16),
            pltpu.VMEM((PEERS, D, ROWS), F32),
            pltpu.VMEM((PEERS, ROWS), F32),
            pltpu.VMEM((PEERS, 8, ROWS), F32),
            pltpu.VMEM((PEERS, ROWS), F32),
            pltpu.VMEM((PEERS, ROWS), F32),
            pltpu.VMEM((PEERS, ROWS), jnp.int32),
            pltpu.VMEM((PEERS, B, G * D), BF16),
            pltpu.VMEM((PEERS, B, G * D), BF16),
            pltpu.VMEM((2, SLOTS) + block, F32),
            pltpu.VMEM((RING, 2, SLOTS) + block, BF16),
            pltpu.VMEM((2, HOPS, CHUNKS) + message, BF16),
            pltpu.VMEM((RING,) + message, BF16),
            dma(peers), dma(peers), dma(peers), dma(peers), dma(hops), dma(hops), dma((RING,)), dma((RING,)),
            dma(peers), dma(peers), dma((RING,)), dma((RING,)), dma(hops), dma(hops), dma((2, PEERS)), dma((2, PEERS)),
            dma((8,)),
        ],
        compiler_params=pltpu.CompilerParams(
            collective_id=0, has_side_effects=True, vmem_limit_bytes=50 * 2**20
        ),
        name="attention",
    )(doc_lengths, queries, keys, values, output_gradient)


def solution(mesh):
    rows = P(("ctx", "head"), None)
    return jax.shard_map(
        shards, mesh=mesh, in_specs=(rows, rows, rows, rows, P()), out_specs=(rows,) * 4, check_vma=False
    )
```

time: 1010 us -> 127 us (0.13)
  the two profiles are of different devices: /device:TPU:4 before, /device:TPU:1 now
where the time goes in v3:
time: 127 us
  Pallas kernels  120 us (94%)
  local copies, waits for them, and re-layouts  5.89 us (5%)
    pallas_call x1, Pallas kernels, shards(): pl.pallas_call(kernel, out_shape=[jax.ShapeDtypeStruct(a.shape, BF16) for...  120 us
    unnamed x10, local copies, waits for them, and re-layouts  5.89 us

profile of v3, /device:TPU:1, one launch (start us, length us, event | category | flops | bytes accessed | tf_op | source)
XLA Modules:
  0.0 126.7 jit_solution(12661140794523896313)
XLA Ops:
  0.6 0.0 copy-start
  0.6 0.9 copy-done
  1.6 0.0 copy-start.1
  1.6 0.9 copy-done.1
  2.5 0.0 copy-start.2
  2.5 0.7 copy-done.2
  3.2 120.1 %attention.1 = (bf16[128,4096]{1,0:T(8,128)(2,1)S(1)}, bf16[128,4096]{1,0:T(8,128)(2,1)S(1)}, bf16[128,1024]{1,0:T(8,128)(2,1)S(1)}, bf16[128,1024]{1,0:T(8,128)(2,1)S(1)}) custom-call(s32[64]{0:T(128)S(1)} %copy-done.2, bf16[128,4096]{1,0:T(8,128)(2,1)} %q_ref.1, bf16[128,1024]{1,0:T(8,128)(2,1)S(1)} %copy-done, bf16[128,1024]{1,0:T(8,128)(2,1)S(1)} %copy-done.1, ...), custom_call_target="tpu_custom_call" | custom-call | tf_op jit(solution)/shard_map/attention/pallas_call | solution.py:436
  123.3 1.0 copy.13
  124.3 1.0 copy.14
  125.3 0.7 copy.15
  126.0 0.7 copy.16
Async XLA Ops:
  0.6 1.0 copy-start
  1.6 0.9 copy-start.1
  2.5 0.7 copy-start.2

commit v4 on v3

--- a/solution.py
+++ b/solution.py
@@ -61,13 +61,15 @@
 
 def kernel(
     length_ref, q_ref, k_ref, v_ref, g_ref, att_out, dq_out, dk_out, dv_out,
-    kv, qs, gs, acc, top, total, shift, delta, starts, atts, dqs, sums, mine, buf, halo_buf,
+    kv, qs, gs, acc, out, top, total, shift, delta, starts, atts, dqs, sums, mine, buf, halo_buf,
     kv_send, kv_recv, row_send, row_recv, ring_send, ring_recv, halo_send, halo_recv,
-    out_send, out_recv, back_send, back_recv, gone_send, gone_recv, last_send, last_recv, own_sem,
+    out_send, out_recv, back_send, back_recv, gone_send, gone_recv, last_send, last_recv, own_sem, lengths, length_sem,
 ):
     ctx, z, group, me = place()
     peers, right, left, above, below = neighbours(ctx, z, group, me)
     base = (group * PEERS - REACH) * SHARD
+    fetch = pltpu.make_async_copy(length_ref, lengths, length_sem)
+    fetch.start()
     enter(peers + [right, left, above, below])
 
     def lanes(head, width):
@@ -87,17 +89,36 @@
             )
         return copies
 
-    key_copies = [
-        copy
+    chip, core = lax.div(me, 2), lax.rem(me, 2)
+    near = (0, 3, 1, 2)
+
+    def key_copy(part, away, other):
+        ref = v_ref if part else k_ref
+        head = 2 * wrap(chip + away, CHUNKS) + other
+        back = (CHUNKS - away) % CHUNKS
+        target = kv.at[part, REACH + me, z]
+        device = (group * PEERS + head, z)
+        sent, come = kv_send.at[part, away, other], kv_recv.at[part, back, core]
+        return (
+            remote(ref.at[:, lanes(head, D)], target, sent, come, device),
+            remote(ref.at[:, lanes(head, D)], target, sent, kv_recv.at[part, away, other], device),
+        )
+
+    def cores_of(away):
+        return (0, 1) if away else (1 - core,)
+
+    own_keys = [
+        pltpu.make_async_copy(ref.at[:, lanes(me, D)], kv.at[part, REACH + me, z], own_sem.at[part])
         for part, ref in enumerate((k_ref, v_ref))
-        for copy in exchange(
-            ref, D, kv.at[part, REACH + me, z], kv_send.at[part], kv_recv.at[part], own_sem.at[part]
-        )
     ]
     query_copies = exchange(q_ref, G * D, qs.at[me], row_send.at[0], row_recv.at[0], own_sem.at[2])
     grad_copies = exchange(g_ref, G * D, gs.at[me], row_send.at[1], row_recv.at[1], own_sem.at[3])
-    for copy in key_copies:
+    for copy in own_keys:
         copy.start()
+    for away in near:
+        for other in cores_of(away):
+            for part in range(2):
+                key_copy(part, away, other)[0].start()
 
     positions = (
         base + REACH * SHARD + z * B
@@ -105,15 +126,22 @@
         + lax.broadcasted_iota(jnp.int32, (PEERS, B), 1)
     )
 
+    fetch.wait()
+
     def one_doc(number, carried):
         start, vector = carried
-        return start + length_ref[number], jnp.where(positions >= start, start, vector)
+        return start + lengths[number], jnp.where(positions >= start, start, vector)
 
     _, vector = lax.fori_loop(
-        0, length_ref.shape[0], one_doc, (jnp.int32(0), jnp.zeros((PEERS, B), jnp.int32))
+        0, lengths.shape[0], one_doc, (jnp.int32(0), jnp.zeros((PEERS, B), jnp.int32))
     )
     starts[...] = jnp.concatenate([vector - base] * G, axis=1)
     token = lax.rem(lax.broadcasted_iota(jnp.int32, (1, ROWS), 1), B)
+
+    def chunk_of(turn):
+        if isinstance(turn, int):
+            return wrap(chip + near[turn], CHUNKS)
+        return wrap(chip + 3 * turn + 3 * lax.div(turn, 2) + 2 * lax.div(turn, 3), CHUNKS)
 
     def ring(way, step, chunk):
         offset = step if way else (RING - step) % RING
@@ -129,9 +157,9 @@
         )
 
     def arrive(step, turn):
-        chunk = CHUNKS - 1 - turn
+        chunk = chunk_of(turn)
         for way in (0, 1):
-            far = (turn < 2) if way else (turn >= 2)
+            far = (turn >= 2) if way else (turn < 2)
             if step < HOPS:
                 ring(way, step - 1, chunk).wait_recv()
             else:
@@ -141,7 +169,7 @@
             elif step == HOPS - 1:
                 pl.when(far)(lambda: ring(way, step, chunk).start())
 
-        @pl.when(turn == 0)
+        @pl.when(chunk == CHUNKS - 1)
         def _():
             halo(step).start()
             if step < HOPS:
@@ -188,13 +216,13 @@
         if offset:
             high = [jnp.maximum(a, b) for a, b in zip(high, before)]
         e = [jnp.exp2((s - h) * (SCALE * LOG2E)) for s, h in zip(found, high)]
-        out = [turned_dot(values_of(i, offset), x.astype(BF16)) for i, x in zip(blocks, e)]
+        found = [turned_dot(values_of(i, offset), x.astype(BF16)) for i, x in zip(blocks, e)]
         count = [fold(x, jnp.sum) for x in e]
         if offset:
             less = [jnp.exp2((b - h) * (SCALE * LOG2E)) for b, h in zip(before, high)]
-            out = [acc[i] * f + o for i, f, o in zip(blocks, less, out)]
+            found = [acc[i] * f + o for i, f, o in zip(blocks, less, found)]
             count = [total[i] * f + c for i, f, c in zip(blocks, less, count)]
-        for i, h, o, c in zip(blocks, high, out, count):
+        for i, h, o, c in zip(blocks, high, found, count):
             top[pl.ds(i, 1), :] = h
             acc[i] = o
             total[i] = c
@@ -216,12 +244,16 @@
 
         lax.fori_loop(0, CHUNKS, turn, 0)
 
-    for copy in key_copies:
+    for copy in own_keys:
         copy.wait()
-    for chunk in reversed(range(CHUNKS)):
+    for turn, away in enumerate(near):
+        for other in cores_of(away):
+            for part in range(2):
+                key_copy(part, away, other)[1].wait_recv()
+        chunk = chunk_of(turn)
         for way in (0, 1):
             ring(way, 0, chunk).start()
-    halo(0).start()
+        pl.when(chunk == CHUNKS - 1)(halo(0).start)
     for copy in query_copies:
         copy.start()
     for k in range(CHUNKS):
@@ -243,27 +275,29 @@
         shift[pl.ds(i, 1), :] = top[pl.ds(i, 1), :] * (SCALE * LOG2E) + jnp.log(count) * LOG2E
         turned = jnp.concatenate([gs[i, :, h * D : (h + 1) * D].astype(F32).T for h in range(G)], axis=1)
         delta[pl.ds(i, 1), :] = jnp.sum(attended * turned, axis=0, keepdims=True)
-        for h in range(G):
-            atts[i, :, h * D : (h + 1) * D] = attended[:, h * B : (h + 1) * B].T.astype(BF16)
+        out[i] = attended.astype(BF16)
         acc[i] = jnp.zeros((D, ROWS), F32)
         return carried
 
     lax.fori_loop(0, PEERS, close, 0)
 
-    def give(ref, out, width, send, recv, own):
-        copies = [pltpu.make_async_copy(ref.at[me], out.at[:, lanes(me, width)], own)]
+    def turn_back(i, carried):
+        for h in range(G):
+            atts[i, :, h * D : (h + 1) * D] = out[i, :, h * B : (h + 1) * B].T
+        return carried
+
+    def give(ref, target, width, send, recv, own):
+        copies = [pltpu.make_async_copy(ref.at[me], target.at[:, lanes(me, width)], own)]
         for d in range(1, PEERS):
             copies.append(
                 remote(
-                    ref.at[wrap(me + d, PEERS)], out.at[:, lanes(me, width)],
+                    ref.at[wrap(me + d, PEERS)], target.at[:, lanes(me, width)],
                     send.at[d - 1], recv.at[d - 1], peers[d - 1],
                 )
             )
         for copy in copies:
             copy.start()
         return copies
-
-    given = give(atts, att_out, G * D, out_send.at[0], out_recv.at[0], own_sem.at[4])
 
     def backward(pair, offset):
         blocks = (2 * pair, 2 * pair + 1)
@@ -290,17 +324,26 @@
         for i, d in zip(blocks, dq):
             acc[i] += d
 
-    def all_backward(offset):
+    def seal(offset, slot, count):
+        for part, scale in enumerate((SCALE, 1.0)):
+            mine[offset, part, slot : slot + count] = (sums[part, slot : slot + count] * scale).astype(BF16)
+
+    def all_backward(offset, hooks=(), early=0):
         sums[...] = jnp.zeros_like(sums)
 
         def one(pair, carried):
+            @pl.when(pair == 1)
+            def _():
+                seal(offset, 0, REACH)
+                home(offset).start()
+
+            for number, hook in hooks:
+                pl.when(pair == number)(hook)
             backward(pair, offset)
             return carried
 
         lax.fori_loop(0, PEERS // 2, one, 0)
-        for part, scale in enumerate((SCALE, 1.0)):
-            mine[offset, part] = (sums[part] * scale).astype(BF16)
-        home(offset).start()
+        seal(offset, REACH + 2 * early, PEERS - 2 * early)
 
     def home(offset):
         return remote(
@@ -336,34 +379,66 @@
                 add(buf.at[way, hops, chunk], piece(chunk, (RING - hops) if way else hops))
             message(way, hops, chunk).start()
 
+    def after_4():
+        add_halo(4)
+        post(1, 4, 3)
+
+    def halo_3():
+        add_halo(3)
+        post(0, 3, 3)
+
+    def early(chunk):
+        def hook():
+            seal(5, REACH + 2 * chunk, 2)
+            post(1, 3, chunk)
+
+        return hook
+
+    def after_5():
+        add_halo(5)
+        post(1, 3, 3)
+
+    def after_2():
+        add_halo(2)
+        post(0, 2, 3)
+
+    def after_6():
+        add_halo(6)
+        post(1, 2, 2)
+
+    def after_1():
+        add_halo(1)
+        post(0, 1, 2)
+
+    def later_1():
+        post(0, 1, 3)
+        post(1, 1, 1)
+
+    def later_7():
+        post(0, 1, 0)
+        post(1, 1, 2)
+
     all_backward(4)
     post(0, 4, 0, 1)
     post(1, 4, 2)
-    all_backward(3)
+    all_backward(3, [(1, after_4)])
     post(0, 3, 2)
-    add_halo(4)
-    post(1, 4, 3)
-    all_backward(5)
-    add_halo(3)
-    post(1, 3, 0, 1)
-    post(0, 3, 3, 0, 1)
+    all_backward(5, [(1, halo_3), (2, early(0)), (3, early(1))], 2)
+    post(0, 3, 0, 1)
     post(1, 3, 2)
-    all_backward(2)
-    add_halo(5)
-    post(1, 3, 3)
+    lax.fori_loop(0, PEERS, turn_back, 0)
+    given = give(atts, att_out, G * D, out_send.at[0], out_recv.at[0], own_sem.at[4])
+    all_backward(2, [(2, after_5)])
     post(0, 2, 2)
-    all_backward(6)
-    add_halo(2)
-    post(0, 2, 3)
-    all_backward(1)
-    add_halo(6)
-    post(0, 2, 0, 1)
-    post(1, 2, 0, 1, 2)
-    all_backward(7)
-    add_halo(1)
+    all_backward(6, [(2, after_2)])
+    post(0, 2, 0)
+    post(1, 2, 0, 1)
+    all_backward(1, [(2, after_6)])
+    post(0, 2, 1)
     post(1, 2, 3)
-    post(0, 1, 2)
-    all_backward(0)
+    all_backward(7, [(2, after_1)])
+    post(1, 1, 0)
+    all_backward(0, [(1, later_1), (3, later_7)])
 
     def close_query(i, carried):
         for h in range(G):
@@ -373,18 +448,14 @@
     lax.fori_loop(0, PEERS, close_query, 0)
     given += give(dqs, dq_out, G * D, out_send.at[1], out_recv.at[1], own_sem.at[5])
     add_halo(7)
+    post(0, 1, 1)
+    post(1, 1, 3)
     add_halo(0)
-    post(0, 1, 3)
-    post(1, 1, 0)
-    post(0, 1, 0)
-    post(1, 1, 1)
-    post(0, 1, 1)
-    post(1, 1, 2, 3)
 
     def last(number, j):
-        out = dv_out if number else dk_out
+        target = dv_out if number else dk_out
         return remote(
-            mine.at[0, number, REACH + j], out.at[:, lanes(me, D)],
+            mine.at[0, number, REACH + j], target.at[:, lanes(me, D)],
             last_send.at[number, j], last_recv.at[number, me], (group * PEERS + j, z),
         )
 
@@ -399,10 +470,10 @@
                 last(0, j).start()
                 last(1, j).start()
 
-    for number, out in enumerate((dk_out, dv_out)):
+    for number, target in enumerate((dk_out, dv_out)):
         given.append(
             pltpu.make_async_copy(
-                mine.at[0, number, REACH + me], out.at[:, lanes(me, D)], own_sem.at[6 + number]
+                mine.at[0, number, REACH + me], target.at[:, lanes(me, D)], own_sem.at[6 + number]
             )
         )
         given[-1].start()
@@ -412,23 +483,28 @@
 
         @pl.when(j != me)
         def _():
-            for number, out in enumerate((dk_out, dv_out)):
+            for number, target in enumerate((dk_out, dv_out)):
                 remote(
-                    mine.at[0, number, REACH + j], out.at[:, lanes(j, D)],
+                    mine.at[0, number, REACH + j], target.at[:, lanes(j, D)],
                     last_send.at[number, j], last_recv.at[number, j], (group * PEERS + j, z),
                 ).wait()
 
     for offset in range(RING):
         halo(offset).wait_send()
         home(offset).wait_send()
+    for away in near:
+        for other in cores_of(away):
+            for part in range(2):
+                key_copy(part, away, other)[0].wait_send()
     for way in (0, 1):
         for chunk in range(CHUNKS):
             for step in range(most(way, chunk)):
-                ring(way, step, chunk).wait_send()
+                ring(way, step, chunk_of(chunk)).wait_send()
                 message(way, step + 1, chunk).wait_send()
 
 
 def shards(queries, keys, values, output_gradient, doc_lengths):
+    arguments = (doc_lengths, queries, keys, values, output_gradient)
     anywhere = pl.BlockSpec(memory_space=pltpu.HBM)
     dma = pltpu.SemaphoreType.DMA
     block, message = (B, D), (2, 2, B, D)
@@ -436,13 +512,14 @@
     return pl.pallas_call(
         kernel,
         out_shape=[jax.ShapeDtypeStruct(a.shape, BF16) for a in (queries, queries, keys, values)],
-        in_specs=[pl.BlockSpec(memory_space=pltpu.SMEM)] + [anywhere] * 4,
+        in_specs=[anywhere] * 5,
         out_specs=[anywhere] * 4,
         scratch_shapes=[
             pltpu.VMEM((2, SLOTS, RING) + block, BF16),
             pltpu.VMEM((PEERS, B, G * D), BF16),
             pltpu.VMEM((PEERS, B, G * D), BF16),
             pltpu.VMEM((PEERS, D, ROWS), F32),
+            pltpu.VMEM((PEERS, D, ROWS), BF16),
             pltpu.VMEM((PEERS, ROWS), F32),
             pltpu.VMEM((PEERS, 8, ROWS), F32),
             pltpu.VMEM((PEERS, ROWS), F32),
@@ -454,15 +531,18 @@
             pltpu.VMEM((RING, 2, SLOTS) + block, BF16),
             pltpu.VMEM((2, HOPS, CHUNKS) + message, BF16),
             pltpu.VMEM((RING,) + message, BF16),
-            dma(peers), dma(peers), dma(peers), dma(peers), dma(hops), dma(hops), dma((RING,)), dma((RING,)),
+            dma((2, CHUNKS, 2)), dma((2, CHUNKS, 2)), dma(peers), dma(peers), dma(hops), dma(hops),
+            dma((RING,)), dma((RING,)),
             dma(peers), dma(peers), dma((RING,)), dma((RING,)), dma(hops), dma(hops), dma((2, PEERS)), dma((2, PEERS)),
             dma((8,)),
+            pltpu.SMEM(doc_lengths.shape, jnp.int32),
+            dma(()),
         ],
         compiler_params=pltpu.CompilerParams(
             collective_id=0, has_side_effects=True, vmem_limit_bytes=50 * 2**20
         ),
         name="attention",
-    )(doc_lengths, queries, keys, values, output_gradient)
+    )(*(pltpu.with_memory_space_constraint(a, pltpu.HBM) for a in arguments))
 
 
 def solution(mesh):

time: 127 us -> 122 us (0.961)
  local copies, waits for them, and re-layouts: 5.89 us -> 3.35 us
  Pallas kernels: 120 us -> 118 us
    pallas_call x1, Pallas kernels: 120 us -> 118 us  [shards(): pl.pallas_call(kernel, out_shape=[jax.ShapeDtypeStruct(a.shape, BF16) for...]
    unnamed x10 -> x4, local copies, waits for them, and re-layouts: 5.89 us -> 3.35 us
where the time goes in v4:
time: 122 us; the launch traced here: 121 us
  Pallas kernels  118 us (97%)
  local copies, waits for them, and re-layouts  3.35 us (3%)
    pallas_call x1, Pallas kernels, shards(): pl.pallas_call(kernel, out_shape=[jax.ShapeDtypeStruct(a.shape, BF16) for...  118 us
    unnamed x4, local copies, waits for them, and re-layouts  3.35 us

profile of v4, /device:TPU:1, one launch (start us, length us, event | category | flops | bytes accessed | tf_op | source)
XLA Modules:
  0.0 121.5 jit_solution(13265765722227072334)
XLA Ops:
  0.6 117.5 %attention.1 = (bf16[128,4096]{1,0:T(8,128)(2,1)S(1)}, bf16[128,4096]{1,0:T(8,128)(2,1)S(1)}, bf16[128,1024]{1,0:T(8,128)(2,1)S(1)}, bf16[128,1024]{1,0:T(8,128)(2,1)S(1)}) custom-call(s32[64]{0:T(128)} %length_ref.1, bf16[128,4096]{1,0:T(8,128)(2,1)} %q_ref.1, bf16[128,1024]{1,0:T(8,128)(2,1)} %k_ref.1, bf16[128,1024]{1,0:T(8,128)(2,1)} %v_ref.1, ...), custom_call_target="tpu_custom_call" | custom-call | tf_op jit(solution)/shard_map/attention/pallas_call | solution.py:512
  118.2 1.0 copy.13
  119.1 1.0 copy.14
  120.1 0.7 copy.15
  120.8 0.7 copy.16

commit v5 on v4

--- a/solution.py
+++ b/solution.py
@@ -160,10 +160,8 @@
         chunk = chunk_of(turn)
         for way in (0, 1):
             far = (turn >= 2) if way else (turn < 2)
-            if step < HOPS:
+            if step < HOPS or far:
                 ring(way, step - 1, chunk).wait_recv()
-            else:
-                pl.when(far)(lambda: ring(way, step - 1, chunk).wait_recv())
             if step < HOPS - 1:
                 ring(way, step, chunk).start()
             elif step == HOPS - 1:
@@ -227,10 +225,12 @@
             acc[i] = o
             total[i] = c
 
-    def four(step, offsets):
+    def four(step, offsets, hooks=()):
         def turn(k, carried):
-            if step is not None:
+            if step is not None and step < HOPS:
                 arrive(step, k)
+            for number, hook in hooks:
+                pl.when(k == number)(hook)
 
             @pl.when(k == CHUNKS - 1)
             def _():
@@ -263,18 +263,31 @@
     for copy in grad_copies:
         copy.start()
     four(2, (0, 7, 1))
-    four(3, (6, 2))
-    four(4, (5, 3))
+
+    def turn_grads():
+        for copy in grad_copies:
+            copy.wait()
+
+        def one(i, carried):
+            for h in range(G):
+                out[i, :, h * B : (h + 1) * B] = gs[i, :, h * D : (h + 1) * D].T
+            return carried
+
+        lax.fori_loop(0, PEERS, one, 0)
+
+    def last_arrivals():
+        for k in (0, 2, 1, 3):
+            arrive(4, k)
+
+    four(3, (6, 2), [(2, turn_grads)])
+    four(4, (5, 3), [(3, last_arrivals)])
     four(None, (4,))
-    for copy in grad_copies:
-        copy.wait()
 
     def close(i, carried):
         count = jnp.sum(total[i], axis=0, keepdims=True)
         attended = (acc[i] * (1.0 / count)).astype(BF16).astype(F32)
         shift[pl.ds(i, 1), :] = top[pl.ds(i, 1), :] * (SCALE * LOG2E) + jnp.log(count) * LOG2E
-        turned = jnp.concatenate([gs[i, :, h * D : (h + 1) * D].astype(F32).T for h in range(G)], axis=1)
-        delta[pl.ds(i, 1), :] = jnp.sum(attended * turned, axis=0, keepdims=True)
+        delta[pl.ds(i, 1), :] = jnp.sum(attended * out[i].astype(F32), axis=0, keepdims=True)
         out[i] = attended.astype(BF16)
         acc[i] = jnp.zeros((D, ROWS), F32)
         return carried

time: 122 us -> 121 us (level)
  no operation moved by 1% of the time
where the time goes in v5:
time: 121 us
  Pallas kernels  117 us (97%)
  local copies, waits for them, and re-layouts  3.35 us (3%)
    pallas_call x1, Pallas kernels, shards(): pl.pallas_call(kernel, out_shape=[jax.ShapeDtypeStruct(a.shape, BF16) for...  117 us
    unnamed x4, local copies, waits for them, and re-layouts  3.35 us

profile of v5, /device:TPU:1, one launch (start us, length us, event | category | flops | bytes accessed | tf_op | source)
XLA Modules:
  0.0 120.6 jit_solution(4765564397706861199)
XLA Ops:
  0.6 116.6 %attention.1 = (bf16[128,4096]{1,0:T(8,128)(2,1)S(1)}, bf16[128,4096]{1,0:T(8,128)(2,1)S(1)}, bf16[128,1024]{1,0:T(8,128)(2,1)S(1)}, bf16[128,1024]{1,0:T(8,128)(2,1)S(1)}) custom-call(s32[64]{0:T(128)} %length_ref.1, bf16[128,4096]{1,0:T(8,128)(2,1)} %q_ref.1, bf16[128,1024]{1,0:T(8,128)(2,1)} %k_ref.1, bf16[128,1024]{1,0:T(8,128)(2,1)} %v_ref.1, ...), custom_call_target="tpu_custom_call" | custom-call | tf_op jit(solution)/shard_map/attention/pallas_call | solution.py:525
  117.2 1.0 copy.13
  118.2 1.0 copy.14
  119.2 0.7 copy.15
  119.9 0.7 copy.16
